TPU v7x, 32 devices: a whole 2x2x4 slice. The times are simulated.
32 devices in a mesh: ctx: 8 (over z, y), head: 4 (over x, core).
Axes of the slice: x: 2, y: 2, z: 4, core: 2. Of those that a mesh axis runs over, the one named last changes fastest.
Arguments:
- features: bfloat16 [8192, 16384], P('ctx', 'head'), may hold values from -6 to 6
- gates: bfloat16 [8192, 16384], P('ctx', 'head'), may hold values from -6 to 6
- state_io: bfloat16 [8192, 2, 2048], P('ctx', None, 'head'), may hold values from -6 to 6
- step_size: float32 [256, 8192], P('head', 'ctx'), may hold values from 0.004 to 0.02
- log_decay: float32 [256, 8192], P('head', 'ctx'), may hold values from -2 to 0, as said below
- conv_feat: bfloat16 [4, 16384], P(None, 'head'), may hold values from -3 to 3
- conv_state: bfloat16 [4, 2, 2048], P(None, None, 'head'), may hold values from -3 to 3
- skip_gain: float32 [256], P('head'), may hold values from 0.5 to 1.5
- norm_gain: float32 [16384], P('head'), may hold values from 0.25 to 1.75
Outputs:
- mixed: bfloat16 [8192, 16384], P(('ctx', 'head'))
Inputs may be any that keep to these rules, and one draw needn't show every extreme that they name: `log_decay`: every entry is negative.
All inputs are finite; a program needn't handle non-finite values.
Results may differ from a plain program's by a relative error of at most 0.0034.
Values may be sent and summed in bfloat16 or wider, within the bound.
No kernel may reach another device: no remote copies, remote signals or barrier semaphores. Data moves between devices by JAX's collectives and lax.ppermute only.
A program may use at most 256 MiB of HBM per device.

v0:
```python
import functools

import jax
import jax.numpy as jnp
import numpy as np
from jax import lax
from jax.experimental import pallas as pl
from jax.experimental.pallas import tpu as pltpu
from jax.sharding import PartitionSpec as P

STATE = 256
SPAN = 128
HALO = 16
EPS = 1e-05
F32 = jnp.float32
BF16 = jnp.bfloat16
VMEM_BYTES = 48 * 1024 * 1024
VMEM_SMALL = 8 * 1024 * 1024
COST = pl.CostEstimate(flops=1, bytes_accessed=1, transcendentals=0)
MSG = STATE + 16
KEPT = STATE + 8


def dot(a, b):
    return jnp.dot(a, b, preferred_element_type=F32)


def silu(v):
    half = 0.5 * v
    return half * jnp.tanh(half) + half


def params(limit=VMEM_BYTES):
    return pltpu.CompilerParams(vmem_limit_bytes=limit)


def spread_table(heads, head_dim):
    head = np.arange(2 * heads) % heads
    return (head[:, None] == (np.arange(heads * head_dim) // head_dim)[None, :]).astype(np.float32)


def decay_kernel(log_ref, step_ref, skip_ref, col_ref, row_ref, loc_ref, dev_ref, ecum_ref, edev_ref, skips_ref):
    heads, tokens = log_ref.shape
    spans = tokens // SPAN
    r = lax.broadcasted_iota(jnp.int32, (SPAN, SPAN), 0)
    c = lax.broadcasted_iota(jnp.int32, (SPAN, SPAN), 1)
    upper = (r <= c).astype(F32)
    cums = []
    for k in range(spans):
        cums.append(
            jnp.dot(
                log_ref[:, k * SPAN : (k + 1) * SPAN],
                upper,
                precision=lax.Precision.HIGHEST,
                preferred_element_type=F32,
            )
        )
    totals = [cum[:, SPAN - 1 :] for cum in cums]
    before = [jnp.zeros_like(totals[0])]
    for k in range(spans - 1):
        before.append(before[-1] + totals[k])
    after = [jnp.zeros_like(totals[0])]
    for k in range(spans - 1, 0, -1):
        after.insert(0, after[0] + totals[k])

    def put(ref, k, value):
        high = value.astype(BF16).astype(F32)
        both = jnp.concatenate([high, value - high], axis=0)
        ref[k * SPAN : (k + 1) * SPAN, :] = both.T.astype(BF16)

    skip = skip_ref[...]
    high = skip.astype(BF16).astype(F32)
    parts = jnp.concatenate([high, skip - high], axis=1)
    skips_ref[...] = jnp.broadcast_to(parts, skips_ref.shape).astype(BF16)
    for k in range(spans):
        cum = cums[k]
        step = step_ref[:, k * SPAN : (k + 1) * SPAN]
        col_ref[k * SPAN : (k + 1) * SPAN, :] = jnp.concatenate([cum, cum], axis=0).T
        row_ref[:, k * SPAN : (k + 1) * SPAN] = cum - jnp.log(step)
        to_end = totals[k] - cum
        put(loc_ref, k, jnp.exp(to_end) * step)
        put(dev_ref, k, jnp.exp(to_end + after[k]) * step)
        put(ecum_ref, k, jnp.exp(cum))
        put(edev_ref, k, jnp.exp(cum + before[k]))


def behind(count):
    return [pl.BlockSpec(memory_space=pl.ANY)] * count


def decay_tables(log_decay, step_size, skip_gain):
    heads, tokens = log_decay.shape
    wide = jax.ShapeDtypeStruct((tokens, 2 * heads), BF16)
    return pl.pallas_call(
        decay_kernel,
        out_shape=(
            jax.ShapeDtypeStruct((tokens, 2 * heads), F32),
            jax.ShapeDtypeStruct((heads, tokens), F32),
            wide,
            wide,
            wide,
            wide,
            jax.ShapeDtypeStruct((16, 2 * heads), BF16),
        ),
        compiler_params=params(VMEM_SMALL),
        name="decays",
        cost_estimate=COST,
    )(log_decay, step_size, skip_gain[None])


def conv_rows(read, rows, halo, taps, store):
    count = taps.shape[0]
    for b in range(rows // SPAN):
        own = read(b * SPAN, (b + 1) * SPAN).astype(F32)
        prev = (halo if b == 0 else read(b * SPAN - HALO, b * SPAN)).astype(F32)
        both = jnp.concatenate([prev[HALO - 8 :], own], axis=0)
        total = own * taps[count - 1 : count]
        for k in range(1, count):
            total = total + both[8 - k : 8 - k + SPAN] * taps[count - 1 - k : count - k]
        store(b, silu(total).astype(BF16))


def read_state(ref):
    if ref.dtype == F32:
        return ref[:STATE, :], ref[STATE : STATE + 1, :]
    tail = ref[STATE:MSG, :].astype(F32)
    return ref[:STATE, :].astype(F32), tail[0:1] + tail[8:9]


def write_kept(ref, value, decay):
    ref[:STATE, :] = value
    ref[STATE:KEPT, :] = jnp.broadcast_to(decay, (KEPT - STATE, decay.shape[1]))


def write_sent(ref, value, decay):
    ref[:STATE, :] = value.astype(BF16)
    high = decay.astype(BF16).astype(F32)
    shape = (8, decay.shape[1])
    rows = jnp.concatenate([jnp.broadcast_to(high, shape), jnp.broadcast_to(decay - high, shape)], axis=0)
    ref[STATE:MSG, :] = rows.astype(BF16)


def maps_kernel(order, io_ref, halo_ref, taps_ref, *refs):
    in_map_ref, out_map_ref, turned_ref = refs[order:]

    def put_in(b, value):
        in_map_ref[b * SPAN : (b + 1) * SPAN, :] = value
        turned_ref[:, b * SPAN : (b + 1) * SPAN] = value.T

    def put_out(b, value):
        out_map_ref[b * SPAN : (b + 1) * SPAN, :] = value

    for i, put in ((0, put_in), (1, put_out)):
        conv_rows(
            lambda lo, hi: io_ref[lo:hi, i, :], io_ref.shape[0], halo_ref[:, i, :],
            taps_ref[:, i, :].astype(F32), put,
        )


def maps_of(group, state_io, halo, conv_state, after):
    tokens = state_io.shape[0]
    count = conv_state.shape[0]

    def mine(j):
        return (0, 0, group)

    return pl.pallas_call(
        functools.partial(maps_kernel, len(after)),
        grid=(1,),
        in_specs=[
            pl.BlockSpec((tokens, 2, STATE), mine),
            pl.BlockSpec((HALO, 2, STATE), mine),
            pl.BlockSpec((count, 2, STATE), mine),
            *behind(len(after)),
        ],
        out_specs=[
            pl.BlockSpec((tokens, STATE), lambda j: (0, 0)),
            pl.BlockSpec((tokens, STATE), lambda j: (0, 0)),
            pl.BlockSpec((STATE, tokens), lambda j: (0, 0)),
        ],
        out_shape=[
            jax.ShapeDtypeStruct((tokens, STATE), BF16),
            jax.ShapeDtypeStruct((tokens, STATE), BF16),
            jax.ShapeDtypeStruct((STATE, tokens), BF16),
        ],
        compiler_params=params(),
        name="maps",
        cost_estimate=COST,
    )(state_io, halo, conv_state, *after)


def front_kernel(order, blocks, where_ref, feat_ref, halo_ref, taps_ref, dev_ref, edev_ref, spread_ref, turned_ref, *refs):
    xh_ref, sent_ref, kept_ref, scaled = refs[order:]
    j = pl.program_id(0)
    spread = spread_ref[...]

    def put_feat(b, value):
        rows = slice(b * SPAN, (b + 1) * SPAN)
        xh_ref[rows, :] = value
        scaled[rows, :] = (value.astype(F32) * dot(dev_ref[rows, :], spread)).astype(BF16)

    conv_rows(
        lambda lo, hi: feat_ref[lo:hi, :], feat_ref.shape[0], halo_ref[...], taps_ref[...].astype(F32), put_feat
    )
    state = dot(turned_ref[...], scaled[...])
    decay = dot(edev_ref[...], spread)[15:16]

    @pl.when(j < blocks)
    def _():
        write_sent(sent_ref, state, decay)

    @pl.when(j >= blocks)
    def _():
        write_kept(kept_ref, state, decay)


def front(chunk, where, features, halo, conv_feat, dev, edev, spread, turned, after):
    tokens = features.shape[0]
    start, width = chunk
    half = width // 2
    block = min(512, half)
    blocks = half // block
    base = start // block
    count = conv_feat.shape[0]
    heads2 = dev.shape[1]

    def place(j, where):
        sending = (j < blocks).astype(jnp.int32)
        which = sending * (1 - where[1]) + (1 - sending) * where[1]
        return which * blocks + j - (1 - sending) * blocks

    def cols(j, where):
        return (0, base + place(j, where))

    def same(j, where):
        return (0, 0)

    return pl.pallas_call(
        functools.partial(front_kernel, len(after), blocks),
        grid_spec=pltpu.PrefetchScalarGridSpec(
            num_scalar_prefetch=1,
            grid=(2 * blocks,),
            in_specs=[
                pl.BlockSpec((tokens, block), cols),
                pl.BlockSpec((HALO, block), cols),
                pl.BlockSpec((count, block), cols),
                pl.BlockSpec((tokens, heads2), same),
                pl.BlockSpec((16, heads2), lambda j, where: (tokens // 16 - 1, 0)),
                pl.BlockSpec((heads2, block), cols),
                pl.BlockSpec((STATE, tokens), same),
                *behind(len(after)),
            ],
            out_specs=[
                pl.BlockSpec((tokens, block), lambda j, where: (0, place(j, where))),
                pl.BlockSpec((MSG, block), lambda j, where: (0, jnp.minimum(j, blocks - 1))),
                pl.BlockSpec((KEPT, block), lambda j, where: (0, jnp.maximum(j - blocks, 0))),
            ],
            scratch_shapes=[pltpu.VMEM((tokens, block), BF16)],
        ),
        out_shape=[
            jax.ShapeDtypeStruct((tokens, width), BF16),
            jax.ShapeDtypeStruct((MSG, half), BF16),
            jax.ShapeDtypeStruct((KEPT, half), F32),
        ],
        compiler_params=params(),
        name="front",
        cost_estimate=COST,
    )(where, features, halo, conv_feat, dev, edev, spread, turned, *after)


def span_kernel(
    first_head, order, xh_ref, in_ref, out_ref, col_ref, row_ref, loc_ref, ecum_ref, spread_ref, skips_ref, halves_ref,
    *refs,
):
    y_ref, state = refs[order:]
    width = xh_ref.shape[1]
    head_dim = width // row_ref.shape[0]

    @pl.when(pl.program_id(0) == 0)
    def _():
        state[...] = jnp.zeros_like(state)

    t = lax.broadcasted_iota(jnp.int32, (SPAN, SPAN), 0)
    s = lax.broadcasted_iota(jnp.int32, (SPAN, SPAN), 1)
    first = halves_ref[0:1, :]
    second = halves_ref[1:2, :]
    block = 256
    for k in range(xh_ref.shape[0] // SPAN):
        rows = slice(k * SPAN, (k + 1) * SPAN)
        in_map = in_ref[rows, :]
        out_map = out_ref[rows, :]
        scores = lax.dot_general(out_map, in_map, (((1,), (1,)), ((), ())), preferred_element_type=F32)
        scores = jnp.where(s <= t, scores, 0.0)
        in_turned = in_map.T
        tables = jnp.concatenate([loc_ref[rows, :], ecum_ref[rows, :], skips_ref[...]], axis=0)
        for q in range(width // block):
            cols = slice(q * block, (q + 1) * block)
            feats = xh_ref[rows, cols]
            feats32 = feats.astype(F32)
            wide = dot(tables, spread_ref[:, cols])
            scaled = (feats32 * wide[:SPAN]).astype(BF16)
            ecum = wide[SPAN : 2 * SPAN]
            skip = wide[2 * SPAN : 2 * SPAN + 1]
            pairs = []
            for p in range(block // 128):
                weights = []
                for i in range(2):
                    h = (q * block + p * 128) // head_dim + i
                    gap = col_ref[rows, first_head + h : first_head + h + 1] - row_ref[h : h + 1, rows]
                    weights.append((scores * jnp.exp(jnp.minimum(gap, 0.0))).astype(BF16))
                pair = feats[:, p * 128 : (p + 1) * 128]
                stacked = jnp.concatenate([pair * first, pair * second], axis=0)
                pairs.append(dot(jnp.concatenate(weights, axis=1), stacked))
            diag = jnp.concatenate(pairs, axis=1)
            held = state[:, cols]
            carried = dot(out_map, held.astype(BF16)) * ecum
            y_ref[rows, cols] = diag + carried + skip * feats32
            state[:, cols] = ecum[SPAN - 1 :] * held + dot(in_turned, scaled)


def spans_of(chunk, head_dim, xh, in_map, out_map, col, row, loc, ecum, spread, skips, halves, after):
    tokens, width = xh.shape
    index = chunk[0] // width
    some = width // head_dim
    heads2 = loc.shape[1]
    tile = 2 * SPAN
    return pl.pallas_call(
        functools.partial(span_kernel, index * some, len(after)),
        grid=(tokens // tile,),
        in_specs=[
            pl.BlockSpec((tile, width), lambda k: (k, 0)),
            pl.BlockSpec((tile, STATE), lambda k: (k, 0)),
            pl.BlockSpec((tile, STATE), lambda k: (k, 0)),
            pl.BlockSpec((tile, heads2), lambda k: (k, 0)),
            pl.BlockSpec((some, tile), lambda k: (index, k)),
            pl.BlockSpec((tile, heads2), lambda k: (k, 0)),
            pl.BlockSpec((tile, heads2), lambda k: (k, 0)),
            pl.BlockSpec((heads2, width), lambda k: (0, index)),
            pl.BlockSpec(skips.shape, lambda k: (0, 0)),
            pl.BlockSpec(halves.shape, lambda k: (0, 0)),
            *behind(len(after)),
        ],
        out_specs=pl.BlockSpec((tile, width), lambda k: (k, 0)),
        out_shape=jax.ShapeDtypeStruct((tokens, width), F32),
        scratch_shapes=[pltpu.VMEM((STATE, width), F32)],
        compiler_params=params(),
        name="spans",
        cost_estimate=COST,
    )(xh, in_map, out_map, col, row, loc, ecum, spread, skips, halves, *after)


def pair_kernel(where_ref, kept_ref, got_ref, *refs):
    total_ref, sent_ref = refs[-2:]
    kept, kept_decay = read_state(kept_ref)
    got, got_decay = read_state(got_ref)

    def put(first, second, decay):
        total = decay * first + second
        write_kept(total_ref, total, kept_decay * got_decay)
        write_sent(sent_ref, total, kept_decay * got_decay)

    @pl.when(where_ref[1] == 0)
    def _():
        put(kept, got, got_decay)

    @pl.when(where_ref[1] == 1)
    def _():
        put(got, kept, kept_decay)


def inclusive_kernel(total_ref, before_ref, *refs):
    sent_ref = refs[-1]
    total, decay = read_state(total_ref)
    before, before_decay = read_state(before_ref)
    write_sent(sent_ref, total + decay * before, decay * before_decay)


def extend_kernel(before_ref, far_ref, *refs):
    before, decay = read_state(before_ref)
    far, far_decay = read_state(far_ref)
    write_kept(refs[-1], before + decay * far, decay * far_decay)


def last_kernel(where_ref, before_ref, far_ref, kept_ref, got_ref, *refs):
    mine_ref, sent_ref = refs[-2:]
    before, before_decay = read_state(before_ref)
    far, _ = read_state(far_ref)
    carried = before + before_decay * far

    @pl.when(where_ref[1] == 0)
    def _():
        kept, decay = read_state(kept_ref)
        mine_ref[...] = carried.astype(BF16)
        sent_ref[...] = (decay * carried + kept).astype(BF16)

    @pl.when(where_ref[1] == 1)
    def _():
        got, decay = read_state(got_ref)
        mine_ref[...] = (decay * carried + got).astype(BF16)
        sent_ref[...] = carried.astype(BF16)


def join(kernel, name, where, operands, outs, after):
    width = operands[0].shape[1]
    shapes = {
        "kept": jax.ShapeDtypeStruct((KEPT, width), F32),
        "sent": jax.ShapeDtypeStruct((MSG, width), BF16),
        "state": jax.ShapeDtypeStruct((STATE, width), BF16),
    }
    scalars = [] if where is None else [where]
    return pl.pallas_call(
        kernel,
        in_specs=[pl.BlockSpec(memory_space=pltpu.SMEM)] * len(scalars)
        + [pl.BlockSpec(memory_space=pltpu.VMEM)] * len(operands)
        + behind(len(after)),
        out_specs=[pl.BlockSpec(memory_space=pltpu.VMEM)] * len(outs),
        out_shape=[shapes[out] for out in outs],
        compiler_params=params(VMEM_SMALL),
        name=name,
        cost_estimate=COST,
    )(*scalars, *operands, *after)


def back_kernel(mode, count, partners, order, where_ref, out_ref, edev_ref, *refs):
    chunks = [refs[6 * i : 6 * i + 6] for i in range(count)]
    refs = refs[6 * count :]
    if mode == "rest":
        squares_ref, *refs = refs
    refs = refs[order:]
    o_refs = refs[:partners]
    if mode == "first":
        squares_ref = refs[partners]
    gated = refs[-1]
    out_map = out_ref[...]
    edev = edev_ref[...]
    rows = out_map.shape[0]
    block = 256
    steps = pl.num_programs(0) // partners
    odd = where_ref[1] == 1
    squares = squares_ref[...] if mode == "rest" else jnp.zeros((rows, 128), F32)
    at = 0
    for y_ref, mine_ref, other_ref, spread_ref, gate_ref, gain_ref in chunks:
        half = mine_ref.shape[1]
        for q in range(2 * half // block):
            cols = slice(q * block, (q + 1) * block)
            inner = slice(q * block % half, q * block % half + block)
            mine = mine_ref[:, inner]
            other = other_ref[:, inner]
            state = jnp.where(odd, other, mine) if q * block < half else jnp.where(odd, mine, other)
            carried = dot(out_map, state) * dot(edev, spread_ref[:, cols])
            value = (y_ref[:, cols] + carried) * silu(gate_ref[:, cols].astype(F32))
            square = value * value
            squares = squares + square[:, :128] + square[:, 128:]
            gated[:, at : at + block] = value * gain_ref[:, cols]
            at += block
    if mode == "first":
        squares_ref[...] = squares
    else:
        width = at if mode == "whole" else 2 * at
        mean = jnp.sum(squares, axis=1, keepdims=True) * (1.0 / width)
        scale = lax.rsqrt(mean + EPS)
    for p in range(partners):

        @pl.when(pl.program_id(0) // steps == p)
        def _(o_ref=o_refs[p]):
            for q in range(at // block):
                cols = slice(q * block, (q + 1) * block)
                value = gated[:, cols] if mode == "first" else gated[:, cols] * scale
                o_ref[:, cols] = value.astype(BF16)
            if mode == "rest":
                high = scale.astype(BF16).astype(F32)
                lane = lax.broadcasted_iota(jnp.int32, (rows, 128), 1)
                o_ref[:, at:] = jnp.where(lane < 64, high, scale - high).astype(BF16)


def back(mode, some, where, rows, chunks, out_map, edev, spread, gates, gain_row, squares, after, own=None):
    heads2 = edev.shape[1]
    tile = 128
    steps = rows // tile
    partners = len(some)

    def at(i, where):
        turn = some[0]
        for p in range(1, partners):
            turn = jnp.where(i >= p * steps, some[p], turn)
        return ((where[0] ^ turn) * steps + i % steps, 0)

    specs = [pl.BlockSpec((tile, STATE), at), pl.BlockSpec((tile, heads2), at)]
    operands = [out_map, edev]
    total = 0
    for (start, width), y, mine, other in chunks:
        index = start // width
        half = width // 2
        total += width
        specs += [
            pl.BlockSpec((tile, width), at),
            pl.BlockSpec((STATE, half), lambda i, where: (0, 0)),
            pl.BlockSpec((STATE, half), lambda i, where: (0, 0)),
            pl.BlockSpec((heads2, width), lambda i, where, index=index: (0, index)),
            pl.BlockSpec((tile, width), lambda i, where, index=index: (at(i, where)[0], index)),
            pl.BlockSpec((1, width), lambda i, where, index=index: (0, index)),
        ]
        operands += [y, mine, other, spread, gates, gain_row]
    if mode == "rest":
        specs.append(pl.BlockSpec((tile, 128), lambda i, where: (i, 0)))
        operands.append(squares)
    aliases = {}
    if own is not None and own[2] is not None:
        after = [own[2], *after]
        aliases = {1 + len(operands): partners - 1}
    specs += behind(len(after))
    operands += after
    sent = total + 128 if mode == "rest" else total

    def part_of(p):
        return lambda i, where: (jnp.clip(i - p * steps, 0, steps - 1), 0)

    out_specs = [pl.BlockSpec((tile, sent), part_of(p)) for p in range(partners)]
    out_shape = [jax.ShapeDtypeStruct((rows, sent), BF16)] * partners
    if own is not None:
        group, groups, _ = own
        out_specs[-1] = pl.BlockSpec(
            (tile, total),
            lambda i, where: (jnp.clip(i - (partners - 1) * steps, 0, steps - 1), (where[0] ^ some[-1]) * groups + group),
        )
        out_shape[-1] = jax.ShapeDtypeStruct((rows, groups * total * (gates.shape[0] // rows)), BF16)
    if mode == "first":
        out_specs.append(pl.BlockSpec((tile, 128), lambda i, where: (i, 0)))
        out_shape.append(jax.ShapeDtypeStruct((partners * rows, 128), F32))
    return pl.pallas_call(
        functools.partial(back_kernel, mode, len(chunks), partners, len(after)),
        grid_spec=pltpu.PrefetchScalarGridSpec(
            num_scalar_prefetch=1,
            grid=(partners * steps,),
            in_specs=specs,
            out_specs=out_specs,
            scratch_shapes=[pltpu.VMEM((tile, total), F32)],
        ),
        out_shape=out_shape,
        input_output_aliases=aliases,
        compiler_params=params(),
        name=f"back_{mode}",
        cost_estimate=COST,
    )(where, *operands)


def shifted(value, pairs, steps):
    return lax.ppermute(
        value,
        "ctx",
        [(2 * q + y, 2 * (q + steps) + y) for q in range(pairs - steps) for y in range(2)],
    )


def swapped(value, pairs):
    return lax.ppermute(value, "ctx", [(2 * q + y, 2 * q + 1 - y) for q in range(pairs) for y in range(2)])


class Line:
    def __init__(self):
        self.last = []

    def run(self, make, *args, **kwargs):
        made = make(*args, after=self.last, **kwargs)
        self.last = [made[0] if isinstance(made, (list, tuple)) else made]
        return made


class Exchange:
    def __init__(self, line, where, pairs, sent, kept):
        self.line = line
        self.where = where
        self.pairs = pairs
        self.kept = kept
        self.got = swapped(sent, pairs)

    def pair(self):
        self.total, sent = self.line.run(
            join, pair_kernel, "pair", self.where, [self.kept, self.got], ["kept", "sent"]
        )
        self.before = shifted(sent, self.pairs, 1)
        self.reach = 1

    def double(self):
        (sent,) = self.line.run(join, inclusive_kernel, "inclusive", None, [self.total, self.before], ["sent"])
        self.far = shifted(sent, self.pairs, self.reach + 1)
        self.reach = 2 * self.reach + 1

    def extend(self):
        while self.reach < self.pairs - 1:
            (self.before,) = self.line.run(join, extend_kernel, "extend", None, [self.before, self.far], ["kept"])
            self.double()

    def finish(self):
        self.extend()
        self.mine, sent = self.line.run(
            join, last_kernel, "last", self.where, [self.before, self.far, self.kept, self.got], ["state", "state"]
        )
        self.other = swapped(sent, self.pairs)


def shards(
    features, gates, state_io, step_size, log_decay, conv_feat, conv_state, skip_gain, norm_gain
):
    tokens, channels = features.shape
    heads = step_size.shape[0]
    head_dim = channels // heads
    groups = state_io.shape[2] // STATE
    group_width = channels // groups
    width = group_width // 2
    count = conv_feat.shape[0]
    rim = count - 1
    ctx_size = lax.axis_size("ctx")
    head_size = lax.axis_size("head")
    pairs = ctx_size // 2
    rows = tokens // head_size
    me = lax.axis_index("head").astype(jnp.int32)
    where = jnp.stack([me, lax.axis_index("ctx").astype(jnp.int32) % 2])

    onward = [(i, i + 1) for i in range(ctx_size - 1)]
    pad = HALO - rim
    halo = jnp.pad(lax.ppermute(features[tokens - rim :], "ctx", onward), ((pad, 0), (0, 0)))
    io_halo = jnp.pad(lax.ppermute(state_io[tokens - rim :], "ctx", onward), ((pad, 0), (0, 0), (0, 0)))
    spread = jnp.asarray(spread_table(heads, head_dim), BF16)
    halves = jnp.asarray(np.arange(128)[None, :] // head_dim == np.arange(2)[:, None], BF16)
    col, row, loc, dev, ecum, edev, skips = decay_tables(log_decay, step_size, skip_gain)
    gain_row = norm_gain[None]

    line = Line()
    chunks = [(c * width, width) for c in range(2 * groups)]
    fronts = {}
    maps = {}
    exchanges = {}
    ys = {}

    def run_maps(g):
        maps[g] = line.run(maps_of, g, state_io, io_halo, conv_state)

    def run_front(c):
        made = line.run(
            front, chunks[c], where, features, halo, conv_feat, dev, edev, spread, maps[c // 2][2]
        )
        fronts[c] = made[0]
        exchanges[c] = Exchange(line, where, pairs, made[1], made[2])

    def run_spans(c):
        g = c // 2
        ys[c] = line.run(
            spans_of, chunks[c], head_dim, fronts[c], *maps[g][:2], col, row, loc, ecum, spread, skips, halves
        )

    def part(c):
        return (chunks[c], ys[c], exchanges[c].mine, exchanges[c].other)

    partners = list(range(head_size - 1, 1, -1))
    squares = {}
    pieces = {}

    def ship(piece, r):
        return lax.ppermute(piece, "head", [(i, i ^ r) for i in range(head_size)])

    def run_back(mode, some, g, parts, squares, own=None):
        return line.run(
            back, mode, some, where, rows, [part(c) for c in parts], maps[g][1], edev, spread, gates, gain_row,
            squares, own=own,
        )

    def arrived(g, index):
        line.last += [pieces[g, r][index] for r in partners]

    def run_first(g, apart=False):
        squares[g] = []
        for some in [[r] for r in partners] if apart else [partners]:
            *made, square = run_back("first", some, g, [2 * g], None)
            squares[g].append((some, square))
            for r, piece in zip(some, made):
                pieces[g, r] = [ship(piece, r)]

    def run_rest(g):
        for some, square in squares[g]:
            made = run_back("rest", some, g, [2 * g + 1], square)
            for r, piece in zip(some, made):
                pieces[g, r].append(ship(piece, r))

    result = None

    def run_near(g):
        nonlocal result
        made, result = run_back("whole", [1, 0], g, [2 * g, 2 * g + 1], None, own=(g, groups, result))
        pieces[g, 1] = [ship(made, 1)]

    def run_put(g, r):
        nonlocal result
        start = (me ^ r) * channels + g * group_width
        zero = jnp.int32(0)
        if len(pieces[g, r]) == 2:
            first, rest = pieces[g, r]
            scale = rest[:, width : width + 1].astype(F32) + rest[:, width + 64 : width + 65].astype(F32)
            first = (first.astype(F32) * scale).astype(BF16)
            result = lax.dynamic_update_slice(result, first, (zero, start))
            result = lax.dynamic_update_slice(result, rest[:, :width], (zero, start + width))
        else:
            result = lax.dynamic_update_slice(result, pieces[g, r][0], (zero, start))

    ex = exchanges
    if groups == 2:
        run_maps(0)
        run_front(0)
        run_front(1)
        ex[0].pair()
        run_maps(1)
        ex[0].double()
        ex[1].pair()
        run_spans(0)
        ex[0].finish()
        ex[1].double()
        run_first(0, apart=True)
        run_front(2)
        run_spans(1)
        ex[1].finish()
        ex[2].pair()
        run_front(3)
        arrived(0, 0)
        run_rest(0)
        ex[2].double()
        ex[3].pair()
        run_spans(2)
        ex[2].finish()
        ex[3].double()
        arrived(0, 1)
        run_first(1)
        run_spans(3)
        ex[3].finish()
        run_near(0)
        arrived(1, 0)
        run_rest(1)
        run_near(1)
    else:
        for c in range(2 * groups):
            if c % 2 == 0:
                run_maps(c // 2)
            run_front(c)
            ex[c].pair()
        for c in range(2 * groups):
            ex[c].double()
            run_spans(c)
        for c in range(2 * groups):
            ex[c].finish()
        for g in range(groups):
            run_first(g)
            run_rest(g)
            run_near(g)
    for g in range(groups):
        run_put(g, 1)
    for g in range(groups):
        for r in partners:
            run_put(g, r)
    return result


def solution(mesh):
    in_specs = (
        P("ctx", "head"),
        P("ctx", "head"),
        P("ctx", None, "head"),
        P("head", "ctx"),
        P("head", "ctx"),
        P(None, "head"),
        P(None, None, "head"),
        P("head"),
        P("head"),
    )
    out_specs = P(("ctx", "head"), None)
    return jax.shard_map(shards, mesh=mesh, in_specs=in_specs, out_specs=out_specs, check_vma=False)
```

profile of v0, /device:TPU:0, one launch (start us, length us, event | category | flops | bytes accessed | tf_op | source)
XLA Modules:
  0.0 232.7 jit_solution(918304741559383077)
XLA Ops:
  0.8 4.9 %collective-permute-start = (bf16[3,2,512]{2,1,0:T(2,128)(2,1)S(1)}, bf16[3,2,512]{2,1,0:T(2,128)(2,1)S(1)}, u32[]{:S(2)}, u32[]{:S(2)}) collective-permute-start(bf16[3,2,512]{2,1,0:T(2,128)(2,1)S(1)} %slice.42), channel_id=1, source_target_pairs={{0,4},{4,8},{8,12},{12,16},{16,20},{20,24},{24,28},{1,5},{5,9},{9,... | collective-permute-start | bytes 18440 | tf_op jit(solution)/shard_map/ppermute | solution.py:623
  6.5 3.4 %collective-permute-start.1 = (bf16[3,4096]{1,0:T(4,128)(2,1)S(1)}, bf16[3,4096]{1,0:T(4,128)(2,1)S(1)}, u32[]{:S(2)}, u32[]{:S(2)}) collective-permute-start(bf16[3,4096]{1,0:T(4,128)(2,1)S(1)} %slice.43), channel_id=1, source_target_pairs={{0,4},{4,8},{8,12},{12,16},{16,20},{20,24},{24,28},{1,5},{5,9},{9,... | collective-permute-start | bytes 73736 | tf_op jit(solution)/shard_map/ppermute | solution.py:622
  15.3 1.7 copy-done.6
  17.7 2.9 %maps.2 = (bf16[1024,256]{1,0:T(8,128)(2,1)S(1)}, bf16[1024,256]{1,0:T(8,128)(2,1)S(1)}, bf16[256,1024]{1,0:T(8,128)(2,1)S(1)}) custom-call(bf16[1024,2,512]{2,1,0:T(2,128)(2,1)S(1)} %copy-done.6, bf16[16,2,512]{2,1,0:T(2,128)(2,1)S(1)} %pad.8.halo_ref, bf16[4,2,512]{2,1,0:T(2,128)(2,1)S(1)} %copy-done.45), custom_call_target="tpu_custom_call" | custom-call | flops 1 | bytes 1 | tf_op jit(solution)/shard_map/maps/pallas_call | solution.py:167
  22.6 6.3 %front.4 = (bf16[1024,1024]{1,0:T(8,128)(2,1)S(1)}, bf16[272,512]{1,0:T(8,128)(2,1)S(1)}, f32[264,512]{1,0:T(8,128)S(1)}) custom-call(s32[2]{0:T(128)S(1)} %pad_add_fusion.where_ref, bf16[1024,4096]{1,0:T(8,128)(2,1)} %feat_ref.7, bf16[16,4096]{1,0:T(8,128)(2,1)S(1)} %pad.9.halo_ref, bf16[4,4096]{1,0:T(4,128)(2,1)S(1)} %copy-done.41, ...), custom_call_target="tpu_custom_call" | custom-call | flops 1 | bytes 1 | tf_op jit(solution)/shard_map/front/pallas_call | solution.py:238
  29.0 1.3 copy-done.10
  31.1 1.5 collective-permute-start.2
  32.6 6.5 %front.5 = (bf16[1024,1024]{1,0:T(8,128)(2,1)S(1)}, bf16[272,512]{1,0:T(8,128)(2,1)S(1)}, f32[264,512]{1,0:T(8,128)S(1)}) custom-call(s32[2]{0:T(128)S(1)} %pad_add_fusion.where_ref, bf16[1024,4096]{1,0:T(8,128)(2,1)} %feat_ref.7, bf16[16,4096]{1,0:T(8,128)(2,1)S(1)} %pad.9.halo_ref, bf16[4,4096]{1,0:T(4,128)(2,1)S(1)} %copy-done.42, ...), custom_call_target="tpu_custom_call" | custom-call | flops 1 | bytes 1 | tf_op jit(solution)/shard_map/front/pallas_call | solution.py:238
  39.9 3.7 %collective-permute-start.4 = (bf16[272,512]{1,0:T(8,128)(2,1)S(1)}, bf16[272,512]{1,0:T(8,128)(2,1)S(1)}, u32[]{:S(2)}, u32[]{:S(2)}) collective-permute-start(bf16[272,512]{1,0:T(8,128)(2,1)S(1)} %get-tuple-element.78), channel_id=1, source_target_pairs={{0,8},{4,12},{8,16},{12,20},{16,24},{20,28},{1,9},{5,13},{9,17},{1... | collective-permute-start | bytes 835592 | tf_op jit(solution)/shard_map/ppermute | solution.py:548
  44.9 2.9 %maps.3 = (bf16[1024,256]{1,0:T(8,128)(2,1)S(1)}, bf16[1024,256]{1,0:T(8,128)(2,1)S(1)}, bf16[256,1024]{1,0:T(8,128)(2,1)S(1)}) custom-call(bf16[1024,2,512]{2,1,0:T(2,128)(2,1)S(1)} %copy-done.7, bf16[16,2,512]{2,1,0:T(2,128)(2,1)S(1)} %pad.8.halo_ref, bf16[4,2,512]{2,1,0:T(2,128)(2,1)S(1)} %copy-done.45, f32[264,512]{1,0:T(8,128)S(1)} %get-tuple-element.67.refs_0_.total_ref), custom_call_target="tpu_custom_call" | custom-call | flops 1 | bytes 1 | tf_op jit(solution)/shard_map/maps/pallas_call | solution.py:167
  48.5 5.4 %collective-permute-start.5 = (bf16[272,512]{1,0:T(8,128)(2,1)S(1)}, bf16[272,512]{1,0:T(8,128)(2,1)S(1)}, u32[]{:S(2)}, u32[]{:S(2)}) collective-permute-start(bf16[272,512]{1,0:T(8,128)(2,1)S(1)} %inclusive.4.refs_0_), channel_id=1, source_target_pairs={{0,16},{4,20},{8,24},{12,28},{1,17},{5,21},{9,25},{13,29},{2,18},{... | collective-permute-start | bytes 835592 | tf_op jit(solution)/shard_map/ppermute | solution.py:548
  54.7 2.2 collective-permute-start.7
  57.0 7.6 %spans.4.refs_0_ = f32[1024,1024]{1,0:T(8,128)} custom-call(bf16[1024,1024]{1,0:T(8,128)(2,1)S(1)} %copy-done.11, bf16[1024,256]{1,0:T(8,128)(2,1)S(1)} %get-tuple-element.62.refs_0_.in_ref, bf16[1024,256]{1,0:T(8,128)(2,1)S(1)} %get-tuple-element.70.out_ref, f32[1024,128]{1,0:T(8,128)S(1)} %get-tuple-element.71.col_ref, ...), custom_call_target="tpu_custom_call" | custom-call | flops 1 | bytes 1 | tf_op jit(solution)/shard_map/spans/pallas_call | solution.py:327
  64.6 2.2 copy-done.2
  68.4 6.2 %collective-permute-start.9 = (bf16[272,512]{1,0:T(8,128)(2,1)S(1)}, bf16[272,512]{1,0:T(8,128)(2,1)S(1)}, u32[]{:S(2)}, u32[]{:S(2)}) collective-permute-start(bf16[272,512]{1,0:T(8,128)(2,1)S(1)} %inclusive.5.refs_6_), channel_id=1, source_target_pairs={{0,16},{4,20},{8,24},{12,28},{1,17},{5,21},{9,25},{13,29},{2,18},{... | collective-permute-start | bytes 835592 | tf_op jit(solution)/shard_map/ppermute | solution.py:548
  74.5 3.1 %back_first.3 = (bf16[256,1024]{1,0:T(8,128)(2,1)}, f32[256,128]{1,0:T(8,128)S(1)}) custom-call(s32[2]{0:T(128)S(1)} %pad_add_fusion.where_ref, bf16[1024,256]{1,0:T(8,128)(2,1)S(1)} %get-tuple-element.70.out_ref, bf16[1024,128]{1,0:T(8,128)(2,1)S(1)} %get-tuple-element.60.edev_ref, f32[1024,1024]{1,0:T(8,128)} %spans.4.refs_0_, ...), custom_call_target="tpu_custom_call" | custom-call | flops 1 | bytes 1 | tf_op jit(solution)/shard_map/back_first/pallas_call | solution.py:530
  77.7 3.1 %back_first.4 = (bf16[256,1024]{1,0:T(8,128)(2,1)}, f32[256,128]{1,0:T(8,128)S(1)}) custom-call(s32[2]{0:T(128)S(1)} %pad_add_fusion.where_ref, bf16[1024,256]{1,0:T(8,128)(2,1)S(1)} %get-tuple-element.70.out_ref, bf16[1024,128]{1,0:T(8,128)(2,1)S(1)} %get-tuple-element.60.edev_ref, f32[1024,1024]{1,0:T(8,128)} %spans.4.refs_0_, ...), custom_call_target="tpu_custom_call" | custom-call | flops 1 | bytes 1 | tf_op jit(solution)/shard_map/back_first/pallas_call | solution.py:530
  80.8 1.5 collective-permute-start.14
  82.3 6.3 %front.6 = (bf16[1024,1024]{1,0:T(8,128)(2,1)S(1)}, bf16[272,512]{1,0:T(8,128)(2,1)S(1)}, f32[264,512]{1,0:T(8,128)S(1)}) custom-call(s32[2]{0:T(128)S(1)} %pad_add_fusion.where_ref, bf16[1024,4096]{1,0:T(8,128)(2,1)} %feat_ref.7, bf16[16,4096]{1,0:T(8,128)(2,1)S(1)} %pad.9.halo_ref, bf16[4,4096]{1,0:T(4,128)(2,1)S(1)} %copy-done.42, ...), custom_call_target="tpu_custom_call" | custom-call | flops 1 | bytes 1 | tf_op jit(solution)/shard_map/front/pallas_call | solution.py:238
  88.7 1.3 copy-done.12
  90.2 7.6 %spans.5.refs_0_.refs_6_ = f32[1024,1024]{1,0:T(8,128)} custom-call(bf16[1024,1024]{1,0:T(8,128)(2,1)S(1)} %get-tuple-element.66.refs_0_.xh_ref, bf16[1024,256]{1,0:T(8,128)(2,1)S(1)} %get-tuple-element.62.refs_0_.in_ref, bf16[1024,256]{1,0:T(8,128)(2,1)S(1)} %get-tuple-element.70.out_ref, f32[1024,128]{1,0:T(8,128)S(1)} %get-tuple-element.71.col_ref, ...), custom_call_target="tpu_custom_call" | custom-call | flops 1 | bytes 1 | tf_op jit(solution)/shard_map/spans/pallas_call | solution.py:327
  97.9 2.2 copy-done.3
  100.8 1.9 collective-permute-start.12
  103.4 2.7 %collective-permute-start.11 = (bf16[272,512]{1,0:T(8,128)(2,1)S(1)}, bf16[272,512]{1,0:T(8,128)(2,1)S(1)}, u32[]{:S(2)}, u32[]{:S(2)}) collective-permute-start(bf16[272,512]{1,0:T(8,128)(2,1)S(1)} %get-tuple-element.93), channel_id=1, source_target_pairs={{0,8},{4,12},{8,16},{12,20},{16,24},{20,28},{1,9},{5,13},{9,17},{1... | collective-permute-start | bytes 835592 | tf_op jit(solution)/shard_map/ppermute | solution.py:548
  106.1 6.3 %front.7 = (bf16[1024,1024]{1,0:T(8,128)(2,1)S(1)}, bf16[272,512]{1,0:T(8,128)(2,1)S(1)}, f32[264,512]{1,0:T(8,128)S(1)}) custom-call(s32[2]{0:T(128)S(1)} %pad_add_fusion.where_ref, bf16[1024,4096]{1,0:T(8,128)(2,1)} %feat_ref.7, bf16[16,4096]{1,0:T(8,128)(2,1)S(1)} %pad.9.halo_ref, bf16[4,4096]{1,0:T(4,128)(2,1)S(1)} %copy-done.42, ...), custom_call_target="tpu_custom_call" | custom-call | flops 1 | bytes 1 | tf_op jit(solution)/shard_map/front/pallas_call | solution.py:238
  112.4 1.3 copy-done.8
  114.8 2.6 %back_rest.3.refs_7_ = bf16[256,1152]{1,0:T(8,128)(2,1)S(1)} custom-call(s32[2]{0:T(128)S(1)} %pad_add_fusion.where_ref, bf16[1024,256]{1,0:T(8,128)(2,1)S(1)} %get-tuple-element.70.out_ref, bf16[1024,128]{1,0:T(8,128)(2,1)S(1)} %get-tuple-element.60.edev_ref, f32[1024,1024]{1,0:T(8,128)} %spans.5.refs_0_.refs_6_, ...), custom_call_target="tpu_custom_call" | custom-call | flops 1 | bytes 1 | tf_op jit(solution)/shard_map/back_rest/pallas_call | solution.py:530
  117.5 2.7 %back_rest.4.refs_0_ = bf16[256,1152]{1,0:T(8,128)(2,1)S(1)} custom-call(s32[2]{0:T(128)S(1)} %pad_add_fusion.where_ref, bf16[1024,256]{1,0:T(8,128)(2,1)S(1)} %get-tuple-element.70.out_ref, bf16[1024,128]{1,0:T(8,128)(2,1)S(1)} %get-tuple-element.60.edev_ref, f32[1024,1024]{1,0:T(8,128)} %spans.5.refs_0_.refs_6_, ...), custom_call_target="tpu_custom_call" | custom-call | flops 1 | bytes 1 | tf_op jit(solution)/shard_map/back_rest/pallas_call | solution.py:530
  121.2 4.6 %collective-permute-start.15 = (bf16[272,512]{1,0:T(8,128)(2,1)S(1)}, bf16[272,512]{1,0:T(8,128)(2,1)S(1)}, u32[]{:S(2)}, u32[]{:S(2)}) collective-permute-start(bf16[272,512]{1,0:T(8,128)(2,1)S(1)} %inclusive.6.refs_0_), channel_id=1, source_target_pairs={{0,16},{4,20},{8,24},{12,28},{1,17},{5,21},{9,25},{13,29},{2,18},{... | collective-permute-start | bytes 835592 | tf_op jit(solution)/shard_map/ppermute | solution.py:548
  126.5 1.6 collective-permute-start.17
  128.1 7.7 %spans.6.refs_0_ = f32[1024,1024]{1,0:T(8,128)} custom-call(bf16[1024,1024]{1,0:T(8,128)(2,1)S(1)} %copy-done.13, bf16[1024,256]{1,0:T(8,128)(2,1)S(1)} %get-tuple-element.79.refs_0_.in_ref, bf16[1024,256]{1,0:T(8,128)(2,1)S(1)} %get-tuple-element.68.out_ref, f32[1024,128]{1,0:T(8,128)S(1)} %get-tuple-element.71.col_ref, ...), custom_call_target="tpu_custom_call" | custom-call | flops 1 | bytes 1 | tf_op jit(solution)/shard_map/spans/pallas_call | solution.py:327
  135.8 2.2 copy-done.4
  138.7 1.8 collective-permute-start.16
  140.6 7.7 %collective-permute-start.20 = (bf16[272,512]{1,0:T(8,128)(2,1)S(1)}, bf16[272,512]{1,0:T(8,128)(2,1)S(1)}, u32[]{:S(2)}, u32[]{:S(2)}) collective-permute-start(bf16[272,512]{1,0:T(8,128)(2,1)S(1)} %inclusive.7.refs_6_), channel_id=1, source_target_pairs={{0,16},{4,20},{8,24},{12,28},{1,17},{5,21},{9,25},{13,29},{2,18},{... | collective-permute-start | bytes 835592 | tf_op jit(solution)/shard_map/ppermute | solution.py:548
  148.4 4.0 %back_first.5 = (bf16[256,1024]{1,0:T(8,128)(2,1)S(1)}, bf16[256,1024]{1,0:T(8,128)(2,1)S(1)}, f32[512,128]{1,0:T(8,128)S(1)}) custom-call(s32[2]{0:T(128)S(1)} %pad_add_fusion.where_ref, bf16[1024,256]{1,0:T(8,128)(2,1)S(1)} %get-tuple-element.68.out_ref, bf16[1024,128]{1,0:T(8,128)(2,1)S(1)} %get-tuple-element.60.edev_ref, f32[1024,1024]{1,0:T(8,128)} %spans.6.refs_0_, ...), custom_call_target="tpu_custom_call" | custom-call | flops 1 | bytes 1 | tf_op jit(solution)/shard_map/back_first/pallas_call | solution.py:530
  153.8 7.6 %spans.7.refs_0_.refs_6_ = f32[1024,1024]{1,0:T(8,128)} custom-call(bf16[1024,1024]{1,0:T(8,128)(2,1)S(1)} %copy-done.9, bf16[1024,256]{1,0:T(8,128)(2,1)S(1)} %get-tuple-element.79.refs_0_.in_ref, bf16[1024,256]{1,0:T(8,128)(2,1)S(1)} %get-tuple-element.68.out_ref, f32[1024,128]{1,0:T(8,128)S(1)} %get-tuple-element.71.col_ref, ...), custom_call_target="tpu_custom_call" | custom-call | flops 1 | bytes 1 | tf_op jit(solution)/shard_map/spans/pallas_call | solution.py:327
  161.4 2.2 copy-done.5
  164.6 6.9 %back_whole.2 = (bf16[256,2048]{1,0:T(8,128)(2,1)}, bf16[256,16384]{1,0:T(8,128)(2,1)}) custom-call(s32[2]{0:T(128)S(1)} %pad_add_fusion.where_ref, bf16[1024,256]{1,0:T(8,128)(2,1)S(1)} %get-tuple-element.70.out_ref, bf16[1024,128]{1,0:T(8,128)(2,1)S(1)} %get-tuple-element.60.edev_ref, f32[1024,1024]{1,0:T(8,128)} %spans.4.refs_0_, ...), custom_call_target="tpu_custom_call" | custom-call | flops 1 | bytes 1 | tf_op jit(solution)/shard_map/back_whole/pallas_call | solution.py:530
  172.0 1.8 collective-permute-start.21
  173.8 6.6 %collective-permute-done.21.refs_2_.refs_8_ = bf16[256,512]{1,0:T(8,128)(2,1)S(1)} collective-permute-done((bf16[256,512]{1,0:T(8,128)(2,1)S(1)}, bf16[256,512]{1,0:T(8,128)(2,1)S(1)}, u32[]{:S(2)}, u32[]{:S(2)}) %collective-permute-start.21) | collective-permute-done | bytes 262176 | tf_op jit(solution)/shard_map/ppermute | solution.py:556
  180.5 5.2 %back_rest.5 = (bf16[256,1152]{1,0:T(8,128)(2,1)}, bf16[256,1152]{1,0:T(8,128)(2,1)S(1)}) custom-call(s32[2]{0:T(128)S(1)} %pad_add_fusion.where_ref, bf16[1024,256]{1,0:T(8,128)(2,1)S(1)} %get-tuple-element.68.out_ref, bf16[1024,128]{1,0:T(8,128)(2,1)S(1)} %get-tuple-element.60.edev_ref, f32[1024,1024]{1,0:T(8,128)} %spans.7.refs_0_.refs_6_, ...), custom_call_target="tpu_custom_call" | custom-call | flops 1 | bytes 1 | tf_op jit(solution)/shard_map/back_rest/pallas_call | solution.py:530
  186.5 6.9 %back_whole.3 = (bf16[256,2048]{1,0:T(8,128)(2,1)}, bf16[256,16384]{1,0:T(8,128)(2,1)}) custom-call(s32[2]{0:T(128)S(1)} %pad_add_fusion.where_ref, bf16[1024,256]{1,0:T(8,128)(2,1)S(1)} %get-tuple-element.68.out_ref, bf16[1024,128]{1,0:T(8,128)(2,1)S(1)} %get-tuple-element.60.edev_ref, ...), custom_call_target="tpu_custom_call", output_to_operand_aliasing={{1}: (15, {})} | custom-call | flops 1 | bytes 1 | tf_op jit(solution)/shard_map/back_whole/pallas_call | solution.py:530
  194.2 1.4 collective-permute-start.27
  196.0 2.3 constant_dynamic-update-slice_fusion.1
  198.3 10.6 %collective-permute-done.26 = bf16[256,1152]{1,0:T(8,128)(2,1)} collective-permute-done((bf16[256,1152]{1,0:T(8,128)(2,1)}, bf16[256,1152]{1,0:T(8,128)(2,1)}, u32[]{:S(2)}, u32[]{:S(2)}) %collective-permute-start.26) | collective-permute-done | bytes 589856 | tf_op jit(solution)/shard_map/ppermute | solution.py:660
  210.0 12.0 %collective-permute-done.27 = bf16[256,1152]{1,0:T(8,128)(2,1)S(1)} collective-permute-done((bf16[256,1152]{1,0:T(8,128)(2,1)}, bf16[256,1152]{1,0:T(8,128)(2,1)S(1)}, u32[]{:S(2)}, u32[]{:S(2)}) %collective-permute-start.27) | collective-permute-done | bytes 589856 | tf_op jit(solution)/shard_map/ppermute | solution.py:660
  222.2 2.3 constant_dynamic-update-slice_fusion
  229.1 1.9 slice_dynamic-update-slice_fusion.1
  (156 shorter events, 33.4 us)
Async XLA Ops:
  0.0 32.6 %copy-start.1 = (bf16[128,4096]{1,0:T(8,128)(2,1)S(1)}, bf16[128,4096]{1,0:T(8,128)(2,1)}, u32[]{:S(2)}) copy-start(bf16[128,4096]{1,0:T(8,128)(2,1)} %constant.53.clone.spread_ref.refs_3_.refs_9_) | copy-start | bytes 3145732
  0.8 14.5 %collective-permute-start = (bf16[3,2,512]{2,1,0:T(2,128)(2,1)S(1)}, bf16[3,2,512]{2,1,0:T(2,128)(2,1)S(1)}, u32[]{:S(2)}, u32[]{:S(2)}) collective-permute-start(bf16[3,2,512]{2,1,0:T(2,128)(2,1)S(1)} %slice.42), channel_id=1, source_target_pairs={{0,4},{4,8},{8,12},{12,16},{16,20},{20,24},{24,28},{1,5},{5,9},{9,... | collective-permute-start | bytes 18440 | tf_op jit(solution)/shard_map/ppermute | solution.py:623
  6.5 14.1 %collective-permute-start.1 = (bf16[3,4096]{1,0:T(4,128)(2,1)S(1)}, bf16[3,4096]{1,0:T(4,128)(2,1)S(1)}, u32[]{:S(2)}, u32[]{:S(2)}) collective-permute-start(bf16[3,4096]{1,0:T(4,128)(2,1)S(1)} %slice.43), channel_id=1, source_target_pairs={{0,4},{4,8},{8,12},{12,16},{16,20},{20,24},{24,28},{1,5},{5,9},{9,... | collective-permute-start | bytes 73736 | tf_op jit(solution)/shard_map/ppermute | solution.py:622
  15.3 23.9 %copy-start.20 = (bf16[1024,128]{1,0:T(8,128)(2,1)}, bf16[1024,128]{1,0:T(8,128)(2,1)S(1)}, u32[]{:S(2)}) copy-start(bf16[1024,128]{1,0:T(8,128)(2,1)S(1)} %get-tuple-element.59.dev_ref) | copy-start | bytes 786436
  17.7 14.9 %copy-start.42 = (bf16[4,4096]{1,0:T(4,128)(2,1)S(1)}, bf16[4,4096]{1,0:T(4,128)(2,1)}, u32[]{:S(2)}) copy-start(bf16[4,4096]{1,0:T(4,128)(2,1)} %taps_ref.11) | copy-start | bytes 98308
  31.1 13.8 %copy-start.7 = (bf16[1024,2,512]{2,1,0:T(2,128)(2,1)S(1)}, bf16[1024,2,512]{2,1,0:T(2,128)(2,1)}, u32[]{:S(2)}) copy-start(bf16[1024,2,512]{2,1,0:T(2,128)(2,1)} %io_ref.3) | copy-start | bytes 6291460
  31.1 8.1 %collective-permute-start.2 = (bf16[272,512]{1,0:T(8,128)(2,1)S(1)}, bf16[272,512]{1,0:T(8,128)(2,1)S(1)}, u32[]{:S(2)}, u32[]{:S(2)}) collective-permute-start(bf16[272,512]{1,0:T(8,128)(2,1)S(1)} %get-tuple-element.64), channel_id=1, source_target_pairs={{0,4},{4,0},{8,12},{12,8},{16,20},{20,16},{24,28},{28,24},{1,5},{5... | collective-permute-start | bytes 835592 | tf_op jit(solution)/shard_map/ppermute | solution.py:556
  32.6 24.3 %copy-start.11 = (bf16[1024,1024]{1,0:T(8,128)(2,1)S(1)}, bf16[1024,1024]{1,0:T(8,128)(2,1)}, u32[]{:S(2)}) copy-start(bf16[1024,1024]{1,0:T(8,128)(2,1)} %copy-done.10) | copy-start | bytes 6291460
  32.6 24.3 %copy-start.15 = (bf16[1024,128]{1,0:T(8,128)(2,1)S(1)}, bf16[1024,128]{1,0:T(8,128)(2,1)}, u32[]{:S(2)}) copy-start(bf16[1024,128]{1,0:T(8,128)(2,1)} %copy-done.14) | copy-start | bytes 786436
  32.6 24.3 %copy-start.18 = (bf16[1024,128]{1,0:T(8,128)(2,1)S(1)}, bf16[1024,128]{1,0:T(8,128)(2,1)}, u32[]{:S(2)}) copy-start(bf16[1024,128]{1,0:T(8,128)(2,1)} %copy-done.17) | copy-start | bytes 786436
  32.6 24.3 %copy-start.46 = (bf16[2,128]{1,0:T(2,128)(2,1)S(1)}, bf16[2,128]{1,0:T(2,128)(2,1)}, u32[]{:S(2)}) copy-start(bf16[2,128]{1,0:T(2,128)(2,1)} %constant.54.clone.halves_ref) | copy-start | bytes 1540
  39.2 25.4 %copy-start.24 = (f32[264,512]{1,0:T(8,128)}, f32[264,512]{1,0:T(8,128)S(1)}, u32[]{:S(2)}) copy-start(f32[264,512]{1,0:T(8,128)S(1)} %get-tuple-element.76.kept_ref) | copy-start | bytes 1622020
  39.9 8.5 %collective-permute-start.4 = (bf16[272,512]{1,0:T(8,128)(2,1)S(1)}, bf16[272,512]{1,0:T(8,128)(2,1)S(1)}, u32[]{:S(2)}, u32[]{:S(2)}) collective-permute-start(bf16[272,512]{1,0:T(8,128)(2,1)S(1)} %get-tuple-element.78), channel_id=1, source_target_pairs={{0,8},{4,12},{8,16},{12,20},{16,24},{20,28},{1,9},{5,13},{9,17},{1... | collective-permute-start | bytes 835592 | tf_op jit(solution)/shard_map/ppermute | solution.py:548
  43.6 10.4 %collective-permute-start.3 = (bf16[272,512]{1,0:T(8,128)(2,1)S(1)}, bf16[272,512]{1,0:T(8,128)(2,1)S(1)}, u32[]{:S(2)}, u32[]{:S(2)}) collective-permute-start(bf16[272,512]{1,0:T(8,128)(2,1)S(1)} %get-tuple-element.77), channel_id=1, source_target_pairs={{0,4},{4,0},{8,12},{12,8},{16,20},{20,16},{24,28},{28,24},{1,5},{5... | collective-permute-start | bytes 835592 | tf_op jit(solution)/shard_map/ppermute | solution.py:556
  48.5 16.0 %collective-permute-start.5 = (bf16[272,512]{1,0:T(8,128)(2,1)S(1)}, bf16[272,512]{1,0:T(8,128)(2,1)S(1)}, u32[]{:S(2)}, u32[]{:S(2)}) collective-permute-start(bf16[272,512]{1,0:T(8,128)(2,1)S(1)} %inclusive.4.refs_0_), channel_id=1, source_target_pairs={{0,16},{4,20},{8,24},{12,28},{1,17},{5,21},{9,25},{13,29},{2,18},{... | collective-permute-start | bytes 835592 | tf_op jit(solution)/shard_map/ppermute | solution.py:548
  54.0 13.5 %copy-start.39 = (bf16[272,512]{1,0:T(8,128)(2,1)}, bf16[272,512]{1,0:T(8,128)(2,1)S(1)}, u32[]{:S(2)}) copy-start(bf16[272,512]{1,0:T(8,128)(2,1)S(1)} %collective-permute-done.3.got_ref) | copy-start | bytes 835588
  54.7 13.6 %collective-permute-start.7 = (bf16[272,512]{1,0:T(8,128)(2,1)S(1)}, bf16[272,512]{1,0:T(8,128)(2,1)S(1)}, u32[]{:S(2)}, u32[]{:S(2)}) collective-permute-start(bf16[272,512]{1,0:T(8,128)(2,1)S(1)} %get-tuple-element.83), channel_id=1, source_target_pairs={{0,8},{4,12},{8,16},{12,20},{16,24},{20,28},{1,9},{5,13},{9,17},{1... | collective-permute-start | bytes 835592 | tf_op jit(solution)/shard_map/ppermute | solution.py:548
  57.0 17.6 %copy-start.36 = (f32[4096]{0:T(1024)S(1)}, f32[4096]{0:T(1024)}, u32[]{:S(2)}) copy-start(f32[4096]{0:T(1024)} %param.19) | copy-start | bytes 49156
  67.5 7.0 %collective-permute-start.6 = (bf16[256,512]{1,0:T(8,128)(2,1)S(1)}, bf16[256,512]{1,0:T(8,128)(2,1)S(1)}, u32[]{:S(2)}, u32[]{:S(2)}) collective-permute-start(bf16[256,512]{1,0:T(8,128)(2,1)S(1)} %get-tuple-element.82), channel_id=1, source_target_pairs={{0,4},{4,0},{8,12},{12,8},{16,20},{20,16},{24,28},{28,24},{1,5},{5... | collective-permute-start | bytes 786440 | tf_op jit(solution)/shard_map/ppermute | solution.py:556
  68.4 29.5 %collective-permute-start.9 = (bf16[272,512]{1,0:T(8,128)(2,1)S(1)}, bf16[272,512]{1,0:T(8,128)(2,1)S(1)}, u32[]{:S(2)}, u32[]{:S(2)}) collective-permute-start(bf16[272,512]{1,0:T(8,128)(2,1)S(1)} %inclusive.5.refs_6_), channel_id=1, source_target_pairs={{0,16},{4,20},{8,24},{12,28},{1,17},{5,21},{9,25},{13,29},{2,18},{... | collective-permute-start | bytes 835592 | tf_op jit(solution)/shard_map/ppermute | solution.py:548
  80.8 33.9 %collective-permute-start.14 = (bf16[256,1024]{1,0:T(8,128)(2,1)}, bf16[256,1024]{1,0:T(8,128)(2,1)S(1)}, u32[]{:S(2)}, u32[]{:S(2)}) collective-permute-start(bf16[256,1024]{1,0:T(8,128)(2,1)} %get-tuple-element.85.refs_0_), channel_id=1, source_target_pairs={{0,2},{1,3},{2,0},{3,1},{4,6},{5,7},{6,4},{7,5},{8,10},{9,11},{10,... | collective-permute-start | bytes 1572872 | tf_op jit(solution)/shard_map/ppermute | solution.py:660
  82.3 32.5 %collective-permute-start.13 = (bf16[256,1024]{1,0:T(8,128)(2,1)}, bf16[256,1024]{1,0:T(8,128)(2,1)S(1)}, u32[]{:S(2)}, u32[]{:S(2)}) collective-permute-start(bf16[256,1024]{1,0:T(8,128)(2,1)} %get-tuple-element.84.refs_6_), channel_id=1, source_target_pairs={{0,3},{1,2},{2,1},{3,0},{4,7},{5,6},{6,5},{7,4},{8,11},{9,10},{10,... | collective-permute-start | bytes 1572872 | tf_op jit(solution)/shard_map/ppermute | solution.py:660
  90.0 12.7 %collective-permute-start.8 = (bf16[272,512]{1,0:T(8,128)(2,1)S(1)}, bf16[272,512]{1,0:T(8,128)(2,1)S(1)}, u32[]{:S(2)}, u32[]{:S(2)}) collective-permute-start(bf16[272,512]{1,0:T(8,128)(2,1)S(1)} %get-tuple-element.88), channel_id=1, source_target_pairs={{0,4},{4,0},{8,12},{12,8},{16,20},{20,16},{24,28},{28,24},{1,5},{5... | collective-permute-start | bytes 835592 | tf_op jit(solution)/shard_map/ppermute | solution.py:556
  100.8 14.0 %collective-permute-start.12 = (bf16[256,512]{1,0:T(8,128)(2,1)S(1)}, bf16[256,512]{1,0:T(8,128)(2,1)S(1)}, u32[]{:S(2)}, u32[]{:S(2)}) collective-permute-start(bf16[256,512]{1,0:T(8,128)(2,1)S(1)} %get-tuple-element.94), channel_id=1, source_target_pairs={{0,4},{4,0},{8,12},{12,8},{16,20},{20,16},{24,28},{28,24},{1,5},{5... | collective-permute-start | bytes 786440 | tf_op jit(solution)/shard_map/ppermute | solution.py:556
  102.7 14.8 %copy-start.37 = (bf16[272,512]{1,0:T(8,128)(2,1)}, bf16[272,512]{1,0:T(8,128)(2,1)S(1)}, u32[]{:S(2)}) copy-start(bf16[272,512]{1,0:T(8,128)(2,1)S(1)} %collective-permute-done.8.got_ref) | copy-start | bytes 835588
  103.4 17.7 %collective-permute-start.11 = (bf16[272,512]{1,0:T(8,128)(2,1)S(1)}, bf16[272,512]{1,0:T(8,128)(2,1)S(1)}, u32[]{:S(2)}, u32[]{:S(2)}) collective-permute-start(bf16[272,512]{1,0:T(8,128)(2,1)S(1)} %get-tuple-element.93), channel_id=1, source_target_pairs={{0,8},{4,12},{8,16},{12,20},{16,24},{20,28},{1,9},{5,13},{9,17},{1... | collective-permute-start | bytes 835592 | tf_op jit(solution)/shard_map/ppermute | solution.py:548
  113.7 12.0 %collective-permute-start.10 = (bf16[272,512]{1,0:T(8,128)(2,1)S(1)}, bf16[272,512]{1,0:T(8,128)(2,1)S(1)}, u32[]{:S(2)}, u32[]{:S(2)}) collective-permute-start(bf16[272,512]{1,0:T(8,128)(2,1)S(1)} %get-tuple-element.92), channel_id=1, source_target_pairs={{0,4},{4,0},{8,12},{12,8},{16,20},{20,16},{24,28},{28,24},{1,5},{5... | collective-permute-start | bytes 835592 | tf_op jit(solution)/shard_map/ppermute | solution.py:556
  117.5 10.6 %copy-start.13 = (bf16[1024,1024]{1,0:T(8,128)(2,1)S(1)}, bf16[1024,1024]{1,0:T(8,128)(2,1)}, u32[]{:S(2)}) copy-start(bf16[1024,1024]{1,0:T(8,128)(2,1)} %copy-done.12) | copy-start | bytes 6291460
  120.2 15.6 %copy-start.38 = (bf16[272,512]{1,0:T(8,128)(2,1)S(1)}, bf16[272,512]{1,0:T(8,128)(2,1)}, u32[]{:S(2)}) copy-start(bf16[272,512]{1,0:T(8,128)(2,1)} %copy-done.37) | copy-start | bytes 835588
  120.2 28.2 %collective-permute-start.19 = (bf16[256,1152]{1,0:T(8,128)(2,1)S(1)}, bf16[256,1152]{1,0:T(8,128)(2,1)S(1)}, u32[]{:S(2)}, u32[]{:S(2)}) collective-permute-start(bf16[256,1152]{1,0:T(8,128)(2,1)S(1)} %back_rest.4.refs_0_), channel_id=1, source_target_pairs={{0,2},{1,3},{2,0},{3,1},{4,6},{5,7},{6,4},{7,5},{8,10},{9,11},{10,... | collective-permute-start | bytes 1769480 | tf_op jit(solution)/shard_map/ppermute | solution.py:660
  120.8 27.6 %collective-permute-start.18 = (bf16[256,1152]{1,0:T(8,128)(2,1)S(1)}, bf16[256,1152]{1,0:T(8,128)(2,1)S(1)}, u32[]{:S(2)}, u32[]{:S(2)}) collective-permute-start(bf16[256,1152]{1,0:T(8,128)(2,1)S(1)} %back_rest.3.refs_7_), channel_id=1, source_target_pairs={{0,3},{1,2},{2,1},{3,0},{4,7},{5,6},{6,5},{7,4},{8,11},{9,10},{10,... | collective-permute-start | bytes 1769480 | tf_op jit(solution)/shard_map/ppermute | solution.py:660
  121.2 14.6 %collective-permute-start.15 = (bf16[272,512]{1,0:T(8,128)(2,1)S(1)}, bf16[272,512]{1,0:T(8,128)(2,1)S(1)}, u32[]{:S(2)}, u32[]{:S(2)}) collective-permute-start(bf16[272,512]{1,0:T(8,128)(2,1)S(1)} %inclusive.6.refs_0_), channel_id=1, source_target_pairs={{0,16},{4,20},{8,24},{12,28},{1,17},{5,21},{9,25},{13,29},{2,18},{... | collective-permute-start | bytes 835592 | tf_op jit(solution)/shard_map/ppermute | solution.py:548
  126.5 14.0 %collective-permute-start.17 = (bf16[272,512]{1,0:T(8,128)(2,1)S(1)}, bf16[272,512]{1,0:T(8,128)(2,1)S(1)}, u32[]{:S(2)}, u32[]{:S(2)}) collective-permute-start(bf16[272,512]{1,0:T(8,128)(2,1)S(1)} %get-tuple-element.101), channel_id=1, source_target_pairs={{0,8},{4,12},{8,16},{12,20},{16,24},{20,28},{1,9},{5,13},{9,17},{1... | collective-permute-start | bytes 835592 | tf_op jit(solution)/shard_map/ppermute | solution.py:548
  138.7 9.7 %collective-permute-start.16 = (bf16[256,512]{1,0:T(8,128)(2,1)S(1)}, bf16[256,512]{1,0:T(8,128)(2,1)S(1)}, u32[]{:S(2)}, u32[]{:S(2)}) collective-permute-start(bf16[256,512]{1,0:T(8,128)(2,1)S(1)} %get-tuple-element.100), channel_id=1, source_target_pairs={{0,4},{4,0},{8,12},{12,8},{16,20},{20,16},{24,28},{28,24},{1,5},{5... | collective-permute-start | bytes 786440 | tf_op jit(solution)/shard_map/ppermute | solution.py:556
  140.6 13.3 %copy-start.9 = (bf16[1024,1024]{1,0:T(8,128)(2,1)S(1)}, bf16[1024,1024]{1,0:T(8,128)(2,1)}, u32[]{:S(2)}) copy-start(bf16[1024,1024]{1,0:T(8,128)(2,1)} %copy-done.8) | copy-start | bytes 6291460
  140.6 13.2 %copy-start.16 = (bf16[1024,128]{1,0:T(8,128)(2,1)S(1)}, bf16[1024,128]{1,0:T(8,128)(2,1)}, u32[]{:S(2)}) copy-start(bf16[1024,128]{1,0:T(8,128)(2,1)} %copy-done.14) | copy-start | bytes 786436
  140.6 20.9 %collective-permute-start.20 = (bf16[272,512]{1,0:T(8,128)(2,1)S(1)}, bf16[272,512]{1,0:T(8,128)(2,1)S(1)}, u32[]{:S(2)}, u32[]{:S(2)}) collective-permute-start(bf16[272,512]{1,0:T(8,128)(2,1)S(1)} %inclusive.7.refs_6_), channel_id=1, source_target_pairs={{0,16},{4,20},{8,24},{12,28},{1,17},{5,21},{9,25},{13,29},{2,18},{... | collective-permute-start | bytes 835592 | tf_op jit(solution)/shard_map/ppermute | solution.py:548
  152.4 28.0 %collective-permute-start.22 = (bf16[256,1024]{1,0:T(8,128)(2,1)S(1)}, bf16[256,1024]{1,0:T(8,128)(2,1)S(1)}, u32[]{:S(2)}, u32[]{:S(2)}) collective-permute-start(bf16[256,1024]{1,0:T(8,128)(2,1)S(1)} %get-tuple-element.102.refs_0_), channel_id=1, source_target_pairs={{0,3},{1,2},{2,1},{3,0},{4,7},{5,6},{6,5},{7,4},{8,11},{9,10},{10,... | collective-permute-start | bytes 1572872 | tf_op jit(solution)/shard_map/ppermute | solution.py:660
  152.6 27.8 %collective-permute-start.23 = (bf16[256,1024]{1,0:T(8,128)(2,1)S(1)}, bf16[256,1024]{1,0:T(8,128)(2,1)S(1)}, u32[]{:S(2)}, u32[]{:S(2)}) collective-permute-start(bf16[256,1024]{1,0:T(8,128)(2,1)S(1)} %get-tuple-element.108), channel_id=1, source_target_pairs={{0,2},{1,3},{2,0},{3,1},{4,6},{5,7},{6,4},{7,5},{8,10},{9,11},{10,... | collective-permute-start | bytes 1572872 | tf_op jit(solution)/shard_map/ppermute | solution.py:660
  171.5 24.5 %collective-permute-start.24 = (bf16[256,2048]{1,0:T(8,128)(2,1)}, bf16[256,2048]{1,0:T(8,128)(2,1)}, u32[]{:S(2)}, u32[]{:S(2)}) collective-permute-start(bf16[256,2048]{1,0:T(8,128)(2,1)} %get-tuple-element.107.refs_7_), channel_id=1, source_target_pairs={{0,1},{1,0},{2,3},{3,2},{4,5},{5,4},{6,7},{7,6},{8,9},{9,8},{10,11... | collective-permute-start | bytes 3145736 | tf_op jit(solution)/shard_map/ppermute | solution.py:660
  172.0 8.4 %collective-permute-start.21 = (bf16[256,512]{1,0:T(8,128)(2,1)S(1)}, bf16[256,512]{1,0:T(8,128)(2,1)S(1)}, u32[]{:S(2)}, u32[]{:S(2)}) collective-permute-start(bf16[256,512]{1,0:T(8,128)(2,1)S(1)} %get-tuple-element.104), channel_id=1, source_target_pairs={{0,4},{4,0},{8,12},{12,8},{16,20},{20,16},{24,28},{28,24},{1,5},{5... | collective-permute-start | bytes 786440 | tf_op jit(solution)/shard_map/ppermute | solution.py:556
  186.5 38.0 %copy-start.31 = (bf16[256,1024]{1,0:T(8,128)(2,1)S(1)}, bf16[256,1024]{1,0:T(8,128)(2,1)}, u32[]{:S(2)}) copy-start(bf16[256,1024]{1,0:T(8,128)(2,1)} %copy-done.30) | copy-start | bytes 1572868
  186.5 39.8 %copy-start.29 = (bf16[256,1024]{1,0:T(8,128)(2,1)S(1)}, bf16[256,1024]{1,0:T(8,128)(2,1)}, u32[]{:S(2)}) copy-start(bf16[256,1024]{1,0:T(8,128)(2,1)} %copy-done.28) | copy-start | bytes 1572868
  193.4 34.7 %copy-start.35 = (bf16[256,1024]{1,0:T(8,128)(2,1)S(1)}, bf16[256,1024]{1,0:T(8,128)(2,1)}, u32[]{:S(2)}) copy-start(bf16[256,1024]{1,0:T(8,128)(2,1)} %copy-done.34) | copy-start | bytes 1572868
  193.4 37.6 %copy-start.33 = (bf16[256,1024]{1,0:T(8,128)(2,1)S(1)}, bf16[256,1024]{1,0:T(8,128)(2,1)}, u32[]{:S(2)}) copy-start(bf16[256,1024]{1,0:T(8,128)(2,1)} %copy-done.32) | copy-start | bytes 1572868
  193.4 28.8 %collective-permute-start.25 = (bf16[256,2048]{1,0:T(8,128)(2,1)}, bf16[256,2048]{1,0:T(8,128)(2,1)}, u32[]{:S(2)}, u32[]{:S(2)}) collective-permute-start(bf16[256,2048]{1,0:T(8,128)(2,1)} %get-tuple-element.111), channel_id=1, source_target_pairs={{0,1},{1,0},{2,3},{3,2},{4,5},{5,4},{6,7},{7,6},{8,9},{9,8},{10,11... | collective-permute-start | bytes 3145736 | tf_op jit(solution)/shard_map/ppermute | solution.py:660
  193.5 15.4 %collective-permute-start.26 = (bf16[256,1152]{1,0:T(8,128)(2,1)}, bf16[256,1152]{1,0:T(8,128)(2,1)}, u32[]{:S(2)}, u32[]{:S(2)}) collective-permute-start(bf16[256,1152]{1,0:T(8,128)(2,1)} %get-tuple-element.109.refs_13_), channel_id=1, source_target_pairs={{0,3},{1,2},{2,1},{3,0},{4,7},{5,6},{6,5},{7,4},{8,11},{9,10},{10,... | collective-permute-start | bytes 1769480 | tf_op jit(solution)/shard_map/ppermute | solution.py:660
  194.2 27.8 %collective-permute-start.27 = (bf16[256,1152]{1,0:T(8,128)(2,1)}, bf16[256,1152]{1,0:T(8,128)(2,1)S(1)}, u32[]{:S(2)}, u32[]{:S(2)}) collective-permute-start(bf16[256,1152]{1,0:T(8,128)(2,1)} %copy-done.48), channel_id=1, source_target_pairs={{0,2},{1,3},{2,0},{3,1},{4,6},{5,7},{6,4},{7,5},{8,10},{9,11},{10,... | collective-permute-start | bytes 1769480 | tf_op jit(solution)/shard_map/ppermute | solution.py:660
  (29 other events, 87.2 us)
where the time goes:
time: 234 us; the launch traced here: 233 us
  Pallas kernels  104 us (44%)
  starting transfers between devices  59.2 us (25%)
  local copies, waits for them, and re-layouts  33.5 us (14%)
  waiting for transfers between devices  30 us (13%)
  other arithmetic  5.47 us (2%)
    pallas_call x8, Pallas kernels, back(): pl.pallas_call(functools.partial(back_kernel, mode, len(chunks), partners...  34.6 us
    ppermute x8, starting transfers between devices, shifted(): lax.ppermute(value, 'ctx', [(2 * q + y, 2 * (q + steps) + y) for q in ran...  34 us
    pallas_call x4, Pallas kernels, spans_of(): pl.pallas_call(functools.partial(span_kernel, index * some, len(after)),...  30.5 us
    pallas_call x4, Pallas kernels, front(): pl.pallas_call(functools.partial(front_kernel, len(after), blocks), grid_...  25.5 us
    unnamed x98, local copies, waits for them, and re-layouts  22.7 us
    ppermute x10, waiting for transfers between devices, ship(): return lax.ppermute(piece, 'head', [(i, i ^ r) for i in range(head_size)])  22.6 us
    ppermute x8, starting transfers between devices, swapped(): lax.ppermute(value, 'ctx', [(2 * q + y, 2 * q + 1 - y) for q in range(pai...  10.3 us
    ppermute x8, waiting for transfers between devices, swapped(): lax.ppermute(value, 'ctx', [(2 * q + y, 2 * q + 1 - y) for q in range(pai...  6.64 us
  transfers between devices with their start and end apart: 28, of which 4 were waited for; matrix products, arithmetic and copies ran while one was open for 2% of the time, Pallas kernels for 42%

commit v1 on v0

--- a/solution.py
+++ b/solution.py
@@ -14,9 +14,9 @@
 EPS = 1e-05
 F32 = jnp.float32
 BF16 = jnp.bfloat16
-VMEM_BYTES = 48 * 1024 * 1024
+VMEM_BYTES = 40 * 1024 * 1024
 VMEM_SMALL = 8 * 1024 * 1024
-COST = pl.CostEstimate(flops=1, bytes_accessed=1, transcendentals=0)
+COST_SCALE = 10**9
 MSG = STATE + 16
 KEPT = STATE + 8
 
@@ -28,6 +28,10 @@
 def silu(v):
     half = 0.5 * v
     return half * jnp.tanh(half) + half
+
+
+def cost(micros):
+    return pl.CostEstimate(flops=int(micros * COST_SCALE), bytes_accessed=1, transcendentals=0)
 
 
 def params(limit=VMEM_BYTES):
@@ -102,9 +106,9 @@
             wide,
             jax.ShapeDtypeStruct((16, 2 * heads), BF16),
         ),
-        compiler_params=params(VMEM_SMALL),
+        compiler_params=params(),
         name="decays",
-        cost_estimate=COST,
+        cost_estimate=cost(1.5),
     )(log_decay, step_size, skip_gain[None])
 
 
@@ -185,7 +189,7 @@
         ],
         compiler_params=params(),
         name="maps",
-        cost_estimate=COST,
+        cost_estimate=cost(3),
     )(state_io, halo, conv_state, *after)
 
 
@@ -264,7 +268,7 @@
         ],
         compiler_params=params(),
         name="front",
-        cost_estimate=COST,
+        cost_estimate=cost(3),
     )(where, features, halo, conv_feat, dev, edev, spread, turned, *after)
 
 
@@ -345,7 +349,7 @@
         scratch_shapes=[pltpu.VMEM((STATE, width), F32)],
         compiler_params=params(),
         name="spans",
-        cost_estimate=COST,
+        cost_estimate=cost(200),
     )(xh, in_map, out_map, col, row, loc, ecum, spread, skips, halves, *after)
 
 
@@ -417,7 +421,7 @@
         out_shape=[shapes[out] for out in outs],
         compiler_params=params(VMEM_SMALL),
         name=name,
-        cost_estimate=COST,
+        cost_estimate=cost(0.7),
     )(*scalars, *operands, *after)
 
 
@@ -463,14 +467,19 @@
 
         @pl.when(pl.program_id(0) // steps == p)
         def _(o_ref=o_refs[p]):
+            if mode == "rest":
+                step = pl.program_id(0) - p * steps
+                start = pl.multiple_of(step * rows, rows)
+                high = scale.astype(BF16).astype(F32)
+                parts = [jnp.broadcast_to(part, (rows, 128)).T[:8] for part in (high, scale - high)]
+                o_ref[steps * rows :, pl.ds(start, rows)] = jnp.concatenate(parts, axis=0).astype(BF16)
             for q in range(at // block):
                 cols = slice(q * block, (q + 1) * block)
                 value = gated[:, cols] if mode == "first" else gated[:, cols] * scale
-                o_ref[:, cols] = value.astype(BF16)
-            if mode == "rest":
-                high = scale.astype(BF16).astype(F32)
-                lane = lax.broadcasted_iota(jnp.int32, (rows, 128), 1)
-                o_ref[:, at:] = jnp.where(lane < 64, high, scale - high).astype(BF16)
+                if mode == "rest":
+                    o_ref[pl.ds(start, rows), cols] = value.astype(BF16)
+                else:
+                    o_ref[:, cols] = value.astype(BF16)
 
 
 def back(mode, some, where, rows, chunks, out_map, edev, spread, gates, gain_row, squares, after, own=None):
@@ -510,13 +519,16 @@
         aliases = {1 + len(operands): partners - 1}
     specs += behind(len(after))
     operands += after
-    sent = total + 128 if mode == "rest" else total
+    sent = rows + 16 if mode == "rest" else rows
+    part = sent if mode == "rest" else tile
 
     def part_of(p):
+        if mode == "rest":
+            return lambda i, where: (0, 0)
         return lambda i, where: (jnp.clip(i - p * steps, 0, steps - 1), 0)
 
-    out_specs = [pl.BlockSpec((tile, sent), part_of(p)) for p in range(partners)]
-    out_shape = [jax.ShapeDtypeStruct((rows, sent), BF16)] * partners
+    out_specs = [pl.BlockSpec((part, total), part_of(p)) for p in range(partners)]
+    out_shape = [jax.ShapeDtypeStruct((sent, total), BF16)] * partners
     if own is not None:
         group, groups, _ = own
         out_specs[-1] = pl.BlockSpec(
@@ -540,7 +552,7 @@
         input_output_aliases=aliases,
         compiler_params=params(),
         name=f"back_{mode}",
-        cost_estimate=COST,
+        cost_estimate=cost(1),
     )(where, *operands)
 
 
@@ -695,10 +707,10 @@
         zero = jnp.int32(0)
         if len(pieces[g, r]) == 2:
             first, rest = pieces[g, r]
-            scale = rest[:, width : width + 1].astype(F32) + rest[:, width + 64 : width + 65].astype(F32)
-            first = (first.astype(F32) * scale).astype(BF16)
+            scale = rest[rows, :rows].astype(F32) + rest[rows + 8, :rows].astype(F32)
+            first = (first.astype(F32) * scale[:, None]).astype(BF16)
             result = lax.dynamic_update_slice(result, first, (zero, start))
-            result = lax.dynamic_update_slice(result, rest[:, :width], (zero, start + width))
+            result = lax.dynamic_update_slice(result, rest[:rows], (zero, start + width))
         else:
             result = lax.dynamic_update_slice(result, pieces[g, r][0], (zero, start))
 
@@ -711,29 +723,29 @@
         run_maps(1)
         ex[0].double()
         ex[1].pair()
+        run_front(2)
         run_spans(0)
         ex[0].finish()
         ex[1].double()
+        ex[2].pair()
         run_first(0, apart=True)
-        run_front(2)
         run_spans(1)
         ex[1].finish()
-        ex[2].pair()
+        ex[2].double()
         run_front(3)
         arrived(0, 0)
         run_rest(0)
-        ex[2].double()
         ex[3].pair()
         run_spans(2)
         ex[2].finish()
         ex[3].double()
+        run_spans(3)
         arrived(0, 1)
         run_first(1)
-        run_spans(3)
         ex[3].finish()
-        run_near(0)
         arrived(1, 0)
         run_rest(1)
+        run_near(0)
         run_near(1)
     else:
         for c in range(2 * groups):
@@ -751,9 +763,7 @@
             run_rest(g)
             run_near(g)
     for g in range(groups):
-        run_put(g, 1)
-    for g in range(groups):
-        for r in partners:
+        for r in [1, *partners]:
             run_put(g, r)
     return result
 

time: 234 us -> 237 us (1.013)
  starting transfers between devices: 59.2 us -> 45.9 us
  local copies, waits for them, and re-layouts: 33.5 us -> 38.4 us
  waiting for transfers between devices: 30 us -> 34.6 us
  Pallas kernels: 104 us -> 107 us
  other arithmetic: 5.47 us -> 8.02 us
    ppermute x8, starting transfers between devices: 34 us -> 22.2 us  [shifted(): lax.ppermute(value, 'ctx', [(2 * q + y, 2 * (q + steps) + y) for q in ran...]
    pallas_call x12, Pallas kernels: 6.28 us -> 17.6 us  [join(): pl.pallas_call(kernel, in_specs=[pl.BlockSpec(memory_space=pltpu.SMEM)] *...]
    pallas_call x4, Pallas kernels: 30.5 us -> 25.9 us  [spans_of(): pl.pallas_call(functools.partial(span_kernel, index * some, len(after)),...]
    unnamed x98 -> x170, local copies, waits for them, and re-layouts: 22.7 us -> 27 us
    ppermute x10, waiting for transfers between devices: 22.6 us -> 25.4 us  [ship(): return lax.ppermute(piece, 'head', [(i, i ^ r) for i in range(head_size)])]
    pallas_call x4, Pallas kernels: 25.5 us -> 23 us  [front(): pl.pallas_call(functools.partial(front_kernel, len(after), blocks), grid_...]
  transfers between devices with their start and end apart: 28 -> 28, of which waited for: 4 -> 5; matrix products, arithmetic and copies ran while one was open for 2% -> 6% of each run, Pallas kernels for 42% -> 39%
where the time goes in v1:
time: 237 us; the launch traced here: 235 us
  Pallas kernels  107 us (45%)
  starting transfers between devices  45.9 us (19%)
  local copies, waits for them, and re-layouts  38.4 us (16%)
  waiting for transfers between devices  34.6 us (15%)
  other arithmetic  8.02 us (3%)
    pallas_call x8, Pallas kernels, back(): pl.pallas_call(functools.partial(back_kernel, mode, len(chunks), partners...  33.8 us
    unnamed x170, local copies, waits for them, and re-layouts  27 us
    pallas_call x4, Pallas kernels, spans_of(): pl.pallas_call(functools.partial(span_kernel, index * some, len(after)),...  25.9 us
    ppermute x10, waiting for transfers between devices, ship(): return lax.ppermute(piece, 'head', [(i, i ^ r) for i in range(head_size)])  25.4 us
    pallas_call x4, Pallas kernels, front(): pl.pallas_call(functools.partial(front_kernel, len(after), blocks), grid_...  23 us
    ppermute x8, starting transfers between devices, shifted(): lax.ppermute(value, 'ctx', [(2 * q + y, 2 * (q + steps) + y) for q in ran...  22.2 us
    pallas_call x12, Pallas kernels, join(): pl.pallas_call(kernel, in_specs=[pl.BlockSpec(memory_space=pltpu.SMEM)] *...  17.6 us
    ppermute x8, starting transfers between devices, swapped(): lax.ppermute(value, 'ctx', [(2 * q + y, 2 * q + 1 - y) for q in range(pai...  8.49 us
  transfers between devices with their start and end apart: 28, of which 5 were waited for; matrix products, arithmetic and copies ran while one was open for 6% of the time, Pallas kernels for 39%

profile of v1, /device:TPU:0, one launch (start us, length us, event | category | flops | bytes accessed | tf_op | source)
XLA Modules:
  0.0 235.3 jit_solution(11132946816746001432)
XLA Ops:
  0.7 4.9 %collective-permute-start = (bf16[3,2,512]{2,1,0:T(2,128)(2,1)S(1)}, bf16[3,2,512]{2,1,0:T(2,128)(2,1)S(1)}, u32[]{:S(2)}, u32[]{:S(2)}) collective-permute-start(bf16[3,2,512]{2,1,0:T(2,128)(2,1)S(1)} %slice.42), channel_id=1, source_target_pairs={{0,4},{4,8},{8,12},{12,16},{16,20},{20,24},{24,28},{1,5},{5,9},{9,... | collective-permute-start | bytes 18440 | tf_op jit(solution)/shard_map/ppermute | solution.py:635
  6.4 3.4 %collective-permute-start.1 = (bf16[3,4096]{1,0:T(4,128)(2,1)S(1)}, bf16[3,4096]{1,0:T(4,128)(2,1)S(1)}, u32[]{:S(2)}, u32[]{:S(2)}) collective-permute-start(bf16[3,4096]{1,0:T(4,128)(2,1)S(1)} %slice.43), channel_id=1, source_target_pairs={{0,4},{4,8},{8,12},{12,16},{16,20},{20,24},{24,28},{1,5},{5,9},{9,... | collective-permute-start | bytes 73736 | tf_op jit(solution)/shard_map/ppermute | solution.py:634
  13.9 2.0 copy-done.62
  16.6 2.9 %maps.2 = (bf16[1024,256]{1,0:T(8,128)(2,1)S(1)}, bf16[1024,256]{1,0:T(8,128)(2,1)S(1)}, bf16[256,1024]{1,0:T(8,128)(2,1)S(1)}) custom-call(bf16[1024,2,512]{2,1,0:T(2,128)(2,1)S(1)} %copy-done.62, bf16[16,2,512]{2,1,0:T(2,128)(2,1)S(1)} %pad.8.halo_ref, bf16[4,2,512]{2,1,0:T(2,128)(2,1)S(1)} %copy-done.71), custom_call_target="tpu_custom_call" | custom-call | flops 3000000000 | bytes 1 | tf_op jit(solution)/shard_map/maps/pallas_call | solution.py:171
  19.5 3.5 %copy-done.1 = bf16[1024,4096]{1,0:T(8,128)(2,1)S(1)} copy-done((bf16[1024,4096]{1,0:T(8,128)(2,1)S(1)}, bf16[1024,4096]{1,0:T(8,128)(2,1)}, u32[]{:S(2)}) %copy-start.1) | copy-done | bytes 8388632
  23.1 5.3 %front.4 = (bf16[1024,1024]{1,0:T(8,128)(2,1)S(1)}, bf16[272,512]{1,0:T(8,128)(2,1)S(1)}, f32[264,512]{1,0:T(8,128)S(1)}) custom-call(s32[2]{0:T(128)S(1)} %pad_add_fusion.where_ref, bf16[1024,4096]{1,0:T(8,128)(2,1)S(1)} %copy-done.1, bf16[16,4096]{1,0:T(8,128)(2,1)S(1)} %pad.9.halo_ref, bf16[4,4096]{1,0:T(4,128)(2,1)S(1)} %copy-done.53, ...), custom_call_target="tpu_custom_call" | custom-call | flops 3000000000 | bytes 1 | tf_op jit(solution)/shard_map/front/pallas_call | solution.py:242
  30.0 6.3 %front.5 = (bf16[1024,1024]{1,0:T(8,128)(2,1)S(1)}, bf16[272,512]{1,0:T(8,128)(2,1)S(1)}, f32[264,512]{1,0:T(8,128)S(1)}) custom-call(s32[2]{0:T(128)S(1)} %pad_add_fusion.where_ref, bf16[1024,4096]{1,0:T(8,128)(2,1)} %feat_ref.7, bf16[16,4096]{1,0:T(8,128)(2,1)S(1)} %pad.9.halo_ref, bf16[4,4096]{1,0:T(4,128)(2,1)S(1)} %copy-done.53, ...), custom_call_target="tpu_custom_call" | custom-call | flops 3000000000 | bytes 1 | tf_op jit(solution)/shard_map/front/pallas_call | solution.py:242
  37.6 3.7 %collective-permute-start.4 = (bf16[272,512]{1,0:T(8,128)(2,1)S(1)}, bf16[272,512]{1,0:T(8,128)(2,1)S(1)}, u32[]{:S(2)}, u32[]{:S(2)}) collective-permute-start(bf16[272,512]{1,0:T(8,128)(2,1)S(1)} %get-tuple-element.72), channel_id=1, source_target_pairs={{0,8},{4,12},{8,16},{12,20},{16,24},{20,28},{1,9},{5,13},{9,17},{1... | collective-permute-start | bytes 835592 | tf_op jit(solution)/shard_map/ppermute | solution.py:560
  41.3 2.9 %maps.3 = (bf16[1024,256]{1,0:T(8,128)(2,1)S(1)}, bf16[1024,256]{1,0:T(8,128)(2,1)S(1)}, bf16[256,1024]{1,0:T(8,128)(2,1)S(1)}) custom-call(bf16[1024,2,512]{2,1,0:T(2,128)(2,1)S(1)} %copy-done.63, bf16[16,2,512]{2,1,0:T(2,128)(2,1)S(1)} %pad.8.halo_ref, bf16[4,2,512]{2,1,0:T(2,128)(2,1)S(1)} %copy-done.71, f32[264,512]{1,0:T(8,128)S(1)} %get-tuple-element.67.refs_0_.total_ref), custom_call_target="tpu_custom_call" | custom-call | flops 3000000000 | bytes 1 | tf_op jit(solution)/shard_map/maps/pallas_call | solution.py:171
  46.7 6.1 %collective-permute-start.7 = (bf16[272,512]{1,0:T(8,128)(2,1)}, bf16[272,512]{1,0:T(8,128)(2,1)}, u32[]{:S(2)}, u32[]{:S(2)}) collective-permute-start(bf16[272,512]{1,0:T(8,128)(2,1)} %inclusive.4.refs_0_), channel_id=1, source_target_pairs={{0,16},{4,20},{8,24},{12,28},{1,17},{5,21},{9,25},{13,29},{2,18},{... | collective-permute-start | bytes 835592 | tf_op jit(solution)/shard_map/ppermute | solution.py:560
  54.3 3.0 %collective-permute-start.6 = (bf16[272,512]{1,0:T(8,128)(2,1)}, bf16[272,512]{1,0:T(8,128)(2,1)}, u32[]{:S(2)}, u32[]{:S(2)}) collective-permute-start(bf16[272,512]{1,0:T(8,128)(2,1)} %get-tuple-element.83), channel_id=1, source_target_pairs={{0,8},{4,12},{8,16},{12,20},{16,24},{20,28},{1,9},{5,13},{9,17},{1... | collective-permute-start | bytes 835592 | tf_op jit(solution)/shard_map/ppermute | solution.py:560
  57.3 3.4 %copy-done.2 = bf16[1024,4096]{1,0:T(8,128)(2,1)S(1)} copy-done((bf16[1024,4096]{1,0:T(8,128)(2,1)S(1)}, bf16[1024,4096]{1,0:T(8,128)(2,1)}, u32[]{:S(2)}) %copy-start.2) | copy-done | bytes 8388632
  60.6 6.0 %front.6 = (bf16[1024,1024]{1,0:T(8,128)(2,1)S(1)}, bf16[272,512]{1,0:T(8,128)(2,1)}, f32[264,512]{1,0:T(8,128)S(1)}) custom-call(s32[2]{0:T(128)S(1)} %pad_add_fusion.where_ref, bf16[1024,4096]{1,0:T(8,128)(2,1)S(1)} %copy-done.2, bf16[16,4096]{1,0:T(8,128)(2,1)S(1)} %pad.9.halo_ref, bf16[4,4096]{1,0:T(4,128)(2,1)S(1)} %copy-done.53, ...), custom_call_target="tpu_custom_call" | custom-call | flops 3000000000 | bytes 1 | tf_op jit(solution)/shard_map/front/pallas_call | solution.py:242
  68.2 6.4 %spans.4.refs_0_ = f32[1024,1024]{1,0:T(8,128)S(1)} custom-call(bf16[1024,1024]{1,0:T(8,128)(2,1)S(1)} %get-tuple-element.65.refs_0_.xh_ref, bf16[1024,256]{1,0:T(8,128)(2,1)S(1)} %get-tuple-element.62.refs_0_.in_ref, bf16[1024,256]{1,0:T(8,128)(2,1)S(1)} %get-tuple-element.84.out_ref, f32[1024,128]{1,0:T(8,128)S(1)} %get-tuple-element.76.col_ref, ...), custom_call_target="tpu_custom_call" | custom-call | flops 199999995904 | bytes 1 | tf_op jit(solution)/shard_map/spans/pallas_call | solution.py:331
  78.5 2.0 collective-permute-start.9
  80.5 1.8 pair.6
  82.4 2.0 collective-permute-start.8
  84.4 3.0 %back_first.3 = (bf16[256,1024]{1,0:T(8,128)(2,1)}, f32[256,128]{1,0:T(8,128)S(1)}) custom-call(s32[2]{0:T(128)S(1)} %copy-done.60, bf16[1024,256]{1,0:T(8,128)(2,1)S(1)} %get-tuple-element.84.out_ref, bf16[1024,128]{1,0:T(8,128)(2,1)S(1)} %get-tuple-element.60.edev_ref, f32[1024,1024]{1,0:T(8,128)S(1)} %spans.4.refs_0_, ...), custom_call_target="tpu_custom_call" | custom-call | flops 1000000000 | bytes 1 | tf_op jit(solution)/shard_map/back_first/pallas_call | solution.py:542
  87.4 3.0 %back_first.4 = (bf16[256,1024]{1,0:T(8,128)(2,1)}, f32[256,128]{1,0:T(8,128)S(1)}) custom-call(s32[2]{0:T(128)S(1)} %copy-done.60, bf16[1024,256]{1,0:T(8,128)(2,1)S(1)} %get-tuple-element.84.out_ref, bf16[1024,128]{1,0:T(8,128)(2,1)S(1)} %get-tuple-element.60.edev_ref, f32[1024,1024]{1,0:T(8,128)S(1)} %spans.4.refs_0_, ...), custom_call_target="tpu_custom_call" | custom-call | flops 1000000000 | bytes 1 | tf_op jit(solution)/shard_map/back_first/pallas_call | solution.py:542
  92.0 6.5 %spans.5.refs_0_.refs_6_ = f32[1024,1024]{1,0:T(8,128)S(1)} custom-call(bf16[1024,1024]{1,0:T(8,128)(2,1)S(1)} %copy-done.34, bf16[1024,256]{1,0:T(8,128)(2,1)S(1)} %get-tuple-element.62.refs_0_.in_ref, bf16[1024,256]{1,0:T(8,128)(2,1)S(1)} %get-tuple-element.84.out_ref, f32[1024,128]{1,0:T(8,128)S(1)} %get-tuple-element.76.col_ref, ...), custom_call_target="tpu_custom_call" | custom-call | flops 199999995904 | bytes 1 | tf_op jit(solution)/shard_map/spans/pallas_call | solution.py:331
  98.5 1.9 last.5
  103.8 3.4 %copy-done.3 = bf16[1024,4096]{1,0:T(8,128)(2,1)S(1)} copy-done((bf16[1024,4096]{1,0:T(8,128)(2,1)S(1)}, bf16[1024,4096]{1,0:T(8,128)(2,1)}, u32[]{:S(2)}) %copy-start.3) | copy-done | bytes 8388632
  107.2 5.3 %front.7 = (bf16[1024,1024]{1,0:T(8,128)(2,1)S(1)}, bf16[272,512]{1,0:T(8,128)(2,1)S(1)}, f32[264,512]{1,0:T(8,128)S(1)}) custom-call(s32[2]{0:T(128)S(1)} %copy-done.60, bf16[1024,4096]{1,0:T(8,128)(2,1)S(1)} %copy-done.3, bf16[16,4096]{1,0:T(8,128)(2,1)S(1)} %copy-done.32, bf16[4,4096]{1,0:T(4,128)(2,1)S(1)} %copy-done.54, ...), custom_call_target="tpu_custom_call" | custom-call | flops 3000000000 | bytes 1 | tf_op jit(solution)/shard_map/front/pallas_call | solution.py:242
  113.1 2.0 collective-permute-start.15
  115.2 3.4 %back_rest.3.refs_7_ = bf16[272,1024]{1,0:T(8,128)(2,1)} custom-call(s32[2]{0:T(128)S(1)} %copy-done.60, bf16[1024,256]{1,0:T(8,128)(2,1)S(1)} %get-tuple-element.84.out_ref, bf16[1024,128]{1,0:T(8,128)(2,1)S(1)} %copy-done.15, f32[1024,1024]{1,0:T(8,128)S(1)} %spans.5.refs_0_.refs_6_, bf16[256,512]{1,0:T(8,128)(2,1)S(1)} %get-tuple-element.91.refs_0_.refs_1_.refs_7_, ...), custom_call_target="tpu_custom_call" | custom-call | flops 1000000000 | bytes 1 | tf_op jit(solution)/shard_map/back_rest/pallas_call | solution.py:542
  119.4 3.7 %back_rest.4.refs_0_ = bf16[272,1024]{1,0:T(8,128)(2,1)} custom-call(s32[2]{0:T(128)S(1)} %copy-done.60, bf16[1024,256]{1,0:T(8,128)(2,1)S(1)} %get-tuple-element.84.out_ref, bf16[1024,128]{1,0:T(8,128)(2,1)S(1)} %copy-done.15, f32[1024,1024]{1,0:T(8,128)S(1)} %spans.5.refs_0_.refs_6_, bf16[256,512]{1,0:T(8,128)(2,1)S(1)} %get-tuple-element.91.refs_0_.refs_1_.refs_7_, ...), custom_call_target="tpu_custom_call" | custom-call | flops 1000000000 | bytes 1 | tf_op jit(solution)/shard_map/back_rest/pallas_call | solution.py:542
  125.0 2.0 collective-permute-start.17
  127.1 6.5 %spans.6.refs_0_ = f32[1024,1024]{1,0:T(8,128)S(1)} custom-call(bf16[1024,1024]{1,0:T(8,128)(2,1)S(1)} %copy-done.65, bf16[1024,256]{1,0:T(8,128)(2,1)S(1)} %copy-done.77, bf16[1024,256]{1,0:T(8,128)(2,1)S(1)} %get-tuple-element.68.out_ref, f32[1024,128]{1,0:T(8,128)S(1)} %copy-done.79, f32[64,1024]{1,0:T(8,128)S(1)} %get-tuple-element.77.row_ref, ...), custom_call_target="tpu_custom_call" | custom-call | flops 199999995904 | bytes 1 | tf_op jit(solution)/shard_map/spans/pallas_call | solution.py:331
  133.6 2.0 last.6
  135.6 2.0 copy-done.8
  140.8 6.5 %spans.7.refs_6_.refs_0_ = f32[1024,1024]{1,0:T(8,128)S(1)} custom-call(bf16[1024,1024]{1,0:T(8,128)(2,1)S(1)} %get-tuple-element.97.refs_7_.xh_ref, bf16[1024,256]{1,0:T(8,128)(2,1)S(1)} %copy-done.77, bf16[1024,256]{1,0:T(8,128)(2,1)S(1)} %get-tuple-element.68.out_ref, f32[1024,128]{1,0:T(8,128)S(1)} %copy-done.79, ...), custom_call_target="tpu_custom_call" | custom-call | flops 199999995904 | bytes 1 | tf_op jit(solution)/shard_map/spans/pallas_call | solution.py:331
  149.8 3.7 %back_first.5 = (bf16[256,1024]{1,0:T(8,128)(2,1)S(1)}, bf16[256,1024]{1,0:T(8,128)(2,1)S(1)}, f32[512,128]{1,0:T(8,128)S(1)}) custom-call(s32[2]{0:T(128)S(1)} %copy-done.60, bf16[1024,256]{1,0:T(8,128)(2,1)S(1)} %get-tuple-element.68.out_ref, bf16[1024,128]{1,0:T(8,128)(2,1)S(1)} %copy-done.15, f32[1024,1024]{1,0:T(8,128)S(1)} %copy-done.9, ...), custom_call_target="tpu_custom_call" | custom-call | flops 1000000000 | bytes 1 | tf_op jit(solution)/shard_map/back_first/pallas_call | solution.py:542
  157.7 7.6 %collective-permute-done.21.refs_2_.refs_8_ = bf16[256,512]{1,0:T(8,128)(2,1)S(1)} collective-permute-done((bf16[256,512]{1,0:T(8,128)(2,1)S(1)}, bf16[256,512]{1,0:T(8,128)(2,1)S(1)}, u32[]{:S(2)}, u32[]{:S(2)}) %collective-permute-start.21) | collective-permute-done | bytes 262176 | tf_op jit(solution)/shard_map/ppermute | solution.py:568
  165.3 2.1 collective-permute-done.22.refs_8_
  167.4 11.6 %collective-permute-done.23.refs_9_ = bf16[256,1024]{1,0:T(8,128)(2,1)S(1)} collective-permute-done((bf16[256,1024]{1,0:T(8,128)(2,1)S(1)}, bf16[256,1024]{1,0:T(8,128)(2,1)S(1)}, u32[]{:S(2)}, u32[]{:S(2)}) %collective-permute-start.23) | collective-permute-done | bytes 524320 | tf_op jit(solution)/shard_map/ppermute | solution.py:672
  179.0 2.2 copy-done.12
  181.2 4.9 %back_rest.5 = (bf16[272,1024]{1,0:T(8,128)(2,1)}, bf16[272,1024]{1,0:T(8,128)(2,1)S(1)}) custom-call(s32[2]{0:T(128)S(1)} %copy-done.60, bf16[1024,256]{1,0:T(8,128)(2,1)S(1)} %get-tuple-element.68.out_ref, bf16[1024,128]{1,0:T(8,128)(2,1)S(1)} %copy-done.16, f32[1024,1024]{1,0:T(8,128)S(1)} %copy-done.12, ...), custom_call_target="tpu_custom_call" | custom-call | flops 1000000000 | bytes 1 | tf_op jit(solution)/shard_map/back_rest/pallas_call | solution.py:542
  186.2 6.3 %back_whole.2 = (bf16[256,2048]{1,0:T(8,128)(2,1)}, bf16[256,16384]{1,0:T(8,128)(2,1)}) custom-call(s32[2]{0:T(128)S(1)} %copy-done.60, bf16[1024,256]{1,0:T(8,128)(2,1)S(1)} %copy-done.18, bf16[1024,128]{1,0:T(8,128)(2,1)S(1)} %copy-done.16, f32[1024,1024]{1,0:T(8,128)S(1)} %copy-done.5, bf16[256,512]{1,0:T(8,128)(2,1)S(1)} %copy-done.20, ...), custom_call_target="tpu_custom_call" | custom-call | flops 1000000000 | bytes 1 | tf_op jit(solution)/shard_map/back_whole/pallas_call | solution.py:542
  196.0 2.2 copy-done.10
  198.2 2.2 copy-done.13
  201.3 5.9 %back_whole.3 = (bf16[256,2048]{1,0:T(8,128)(2,1)S(1)}, bf16[256,16384]{1,0:T(8,128)(2,1)}) custom-call(s32[2]{0:T(128)S(1)} %copy-done.61, bf16[1024,256]{1,0:T(8,128)(2,1)S(1)} %get-tuple-element.68.out_ref, bf16[1024,128]{1,0:T(8,128)(2,1)S(1)} %copy-done.16, f32[1024,1024]{1,0:T(8,128)S(1)} %copy-done.10, ...), custom_call_target="tpu_custom_call", output_to_operand_aliasing={{1}: (15, {})} | custom-call | flops 1000000000 | bytes 1 | tf_op jit(solution)/shard_map/back_whole/pallas_call | solution.py:542
  207.9 11.7 %collective-permute-done.27 = bf16[272,1024]{1,0:T(8,128)(2,1)S(1)} collective-permute-done((bf16[272,1024]{1,0:T(8,128)(2,1)}, bf16[272,1024]{1,0:T(8,128)(2,1)S(1)}, u32[]{:S(2)}, u32[]{:S(2)}) %collective-permute-start.27) | collective-permute-done | bytes 557088 | tf_op jit(solution)/shard_map/ppermute | solution.py:672
  219.6 2.3 constant_dynamic-update-slice_fusion.1
  221.9 2.0 fusion
  223.9 1.9 slice_dynamic-update-slice_fusion.3
  225.8 2.0 fusion.1
  227.8 1.9 slice_dynamic-update-slice_fusion.2
  231.7 1.9 slice_dynamic-update-slice_fusion.1
  (228 shorter events, 45.3 us)
Async XLA Ops:
  0.7 13.1 %collective-permute-start = (bf16[3,2,512]{2,1,0:T(2,128)(2,1)S(1)}, bf16[3,2,512]{2,1,0:T(2,128)(2,1)S(1)}, u32[]{:S(2)}, u32[]{:S(2)}) collective-permute-start(bf16[3,2,512]{2,1,0:T(2,128)(2,1)S(1)} %slice.42), channel_id=1, source_target_pairs={{0,4},{4,8},{8,12},{12,16},{16,20},{20,24},{24,28},{1,5},{5,9},{9,... | collective-permute-start | bytes 18440 | tf_op jit(solution)/shard_map/ppermute | solution.py:635
  6.4 13.0 %collective-permute-start.1 = (bf16[3,4096]{1,0:T(4,128)(2,1)S(1)}, bf16[3,4096]{1,0:T(4,128)(2,1)S(1)}, u32[]{:S(2)}, u32[]{:S(2)}) collective-permute-start(bf16[3,4096]{1,0:T(4,128)(2,1)S(1)} %slice.43), channel_id=1, source_target_pairs={{0,4},{4,8},{8,12},{12,16},{16,20},{20,24},{24,28},{1,5},{5,9},{9,... | collective-permute-start | bytes 73736 | tf_op jit(solution)/shard_map/ppermute | solution.py:634
  13.7 43.6 %copy-start.27 = (bf16[1024,128]{1,0:T(8,128)(2,1)}, bf16[1024,128]{1,0:T(8,128)(2,1)S(1)}, u32[]{:S(2)}) copy-start(bf16[1024,128]{1,0:T(8,128)(2,1)S(1)} %get-tuple-element.59.dev_ref) | copy-start | bytes 786436
  13.7 54.5 %copy-start.82 = (bf16[1024,128]{1,0:T(8,128)(2,1)}, bf16[1024,128]{1,0:T(8,128)(2,1)S(1)}, u32[]{:S(2)}) copy-start(bf16[1024,128]{1,0:T(8,128)(2,1)S(1)} %get-tuple-element.79.ecum_ref) | copy-start | bytes 786436
  13.7 73.6 %copy-start.14 = (bf16[1024,128]{1,0:T(8,128)(2,1)}, bf16[1024,128]{1,0:T(8,128)(2,1)S(1)}, u32[]{:S(2)}) copy-start(bf16[1024,128]{1,0:T(8,128)(2,1)S(1)} %get-tuple-element.60.edev_ref) | copy-start | bytes 786436
  13.7 78.2 %copy-start.78 = (f32[1024,128]{1,0:T(8,128)}, f32[1024,128]{1,0:T(8,128)S(1)}, u32[]{:S(2)}) copy-start(f32[1024,128]{1,0:T(8,128)S(1)} %get-tuple-element.76.col_ref) | copy-start | bytes 1572868
  13.7 78.2 %copy-start.80 = (bf16[1024,128]{1,0:T(8,128)(2,1)}, bf16[1024,128]{1,0:T(8,128)(2,1)S(1)}, u32[]{:S(2)}) copy-start(bf16[1024,128]{1,0:T(8,128)(2,1)S(1)} %get-tuple-element.78.loc_ref) | copy-start | bytes 786436
  13.8 43.4 %copy-start.59 = (s32[2]{0:T(128)}, s32[2]{0:T(128)S(1)}, u32[]{:S(2)}) copy-start(s32[2]{0:T(128)S(1)} %pad_add_fusion.where_ref) | copy-start | bytes 28
  19.4 99.9 %copy-start.17 = (bf16[1024,256]{1,0:T(8,128)(2,1)}, bf16[1024,256]{1,0:T(8,128)(2,1)S(1)}, u32[]{:S(2)}) copy-start(bf16[1024,256]{1,0:T(8,128)(2,1)S(1)} %get-tuple-element.84.out_ref) | copy-start | bytes 1572868
  19.5 37.8 %copy-start.31 = (bf16[16,4096]{1,0:T(8,128)(2,1)}, bf16[16,4096]{1,0:T(8,128)(2,1)S(1)}, u32[]{:S(2)}) copy-start(bf16[16,4096]{1,0:T(8,128)(2,1)S(1)} %pad.9.halo_ref) | copy-start | bytes 393220
  28.4 8.5 %collective-permute-start.2 = (bf16[272,512]{1,0:T(8,128)(2,1)S(1)}, bf16[272,512]{1,0:T(8,128)(2,1)S(1)}, u32[]{:S(2)}, u32[]{:S(2)}) collective-permute-start(bf16[272,512]{1,0:T(8,128)(2,1)S(1)} %get-tuple-element.64), channel_id=1, source_target_pairs={{0,4},{4,0},{8,12},{12,8},{16,20},{20,16},{24,28},{28,24},{1,5},{5... | collective-permute-start | bytes 835592 | tf_op jit(solution)/shard_map/ppermute | solution.py:568
  36.3 16.5 %collective-permute-start.3 = (bf16[272,512]{1,0:T(8,128)(2,1)S(1)}, bf16[272,512]{1,0:T(8,128)(2,1)S(1)}, u32[]{:S(2)}, u32[]{:S(2)}) collective-permute-start(bf16[272,512]{1,0:T(8,128)(2,1)S(1)} %get-tuple-element.71), channel_id=1, source_target_pairs={{0,4},{4,0},{8,12},{12,8},{16,20},{20,16},{24,28},{28,24},{1,5},{5... | collective-permute-start | bytes 835592 | tf_op jit(solution)/shard_map/ppermute | solution.py:568
  37.6 8.3 %collective-permute-start.4 = (bf16[272,512]{1,0:T(8,128)(2,1)S(1)}, bf16[272,512]{1,0:T(8,128)(2,1)S(1)}, u32[]{:S(2)}, u32[]{:S(2)}) collective-permute-start(bf16[272,512]{1,0:T(8,128)(2,1)S(1)} %get-tuple-element.72), channel_id=1, source_target_pairs={{0,8},{4,12},{8,16},{12,20},{16,24},{20,28},{1,9},{5,13},{9,17},{1... | collective-permute-start | bytes 835592 | tf_op jit(solution)/shard_map/ppermute | solution.py:560
  44.2 23.9 %copy-start.51 = (bf16[256,1024]{1,0:T(8,128)(2,1)}, bf16[256,1024]{1,0:T(8,128)(2,1)S(1)}, u32[]{:S(2)}) copy-start(bf16[256,1024]{1,0:T(8,128)(2,1)S(1)} %get-tuple-element.69.turned_ref) | copy-start | bytes 1572868
  44.2 23.9 %copy-start.76 = (bf16[1024,256]{1,0:T(8,128)(2,1)}, bf16[1024,256]{1,0:T(8,128)(2,1)S(1)}, u32[]{:S(2)}) copy-start(bf16[1024,256]{1,0:T(8,128)(2,1)S(1)} %get-tuple-element.73.refs_0_.in_ref) | copy-start | bytes 1572868
  44.2 23.9 %copy-start.73 = (bf16[2,128]{1,0:T(2,128)(2,1)S(1)}, bf16[2,128]{1,0:T(2,128)(2,1)}, u32[]{:S(2)}) copy-start(bf16[2,128]{1,0:T(2,128)(2,1)} %constant.54.clone.halves_ref) | copy-start | bytes 1540
  45.9 22.3 %copy-start.57 = (bf16[272,512]{1,0:T(8,128)(2,1)}, bf16[272,512]{1,0:T(8,128)(2,1)S(1)}, u32[]{:S(2)}) copy-start(bf16[272,512]{1,0:T(8,128)(2,1)S(1)} %collective-permute-done.4.before_ref) | copy-start | bytes 835588
  46.7 28.0 %collective-permute-start.7 = (bf16[272,512]{1,0:T(8,128)(2,1)}, bf16[272,512]{1,0:T(8,128)(2,1)}, u32[]{:S(2)}, u32[]{:S(2)}) collective-permute-start(bf16[272,512]{1,0:T(8,128)(2,1)} %inclusive.4.refs_0_), channel_id=1, source_target_pairs={{0,16},{4,20},{8,24},{12,28},{1,17},{5,21},{9,25},{13,29},{2,18},{... | collective-permute-start | bytes 835592 | tf_op jit(solution)/shard_map/ppermute | solution.py:560
  54.3 22.5 %collective-permute-start.6 = (bf16[272,512]{1,0:T(8,128)(2,1)}, bf16[272,512]{1,0:T(8,128)(2,1)}, u32[]{:S(2)}, u32[]{:S(2)}) collective-permute-start(bf16[272,512]{1,0:T(8,128)(2,1)} %get-tuple-element.83), channel_id=1, source_target_pairs={{0,8},{4,12},{8,16},{12,20},{16,24},{20,28},{1,9},{5,13},{9,17},{1... | collective-permute-start | bytes 835592 | tf_op jit(solution)/shard_map/ppermute | solution.py:560
  66.7 13.9 %collective-permute-start.5 = (bf16[272,512]{1,0:T(8,128)(2,1)}, bf16[272,512]{1,0:T(8,128)(2,1)}, u32[]{:S(2)}, u32[]{:S(2)}) collective-permute-start(bf16[272,512]{1,0:T(8,128)(2,1)} %get-tuple-element.82), channel_id=1, source_target_pairs={{0,4},{4,0},{8,12},{12,8},{16,20},{20,16},{24,28},{28,24},{1,5},{5... | collective-permute-start | bytes 835592 | tf_op jit(solution)/shard_map/ppermute | solution.py:568
  76.1 8.2 %collective-permute-start.10 = (bf16[256,512]{1,0:T(8,128)(2,1)S(1)}, bf16[256,512]{1,0:T(8,128)(2,1)S(1)}, u32[]{:S(2)}, u32[]{:S(2)}) collective-permute-start(bf16[256,512]{1,0:T(8,128)(2,1)S(1)} %get-tuple-element.88), channel_id=1, source_target_pairs={{0,4},{4,0},{8,12},{12,8},{16,20},{20,16},{24,28},{28,24},{1,5},{5... | collective-permute-start | bytes 786440 | tf_op jit(solution)/shard_map/ppermute | solution.py:568
  78.5 20.0 %collective-permute-start.9 = (bf16[272,512]{1,0:T(8,128)(2,1)}, bf16[272,512]{1,0:T(8,128)(2,1)}, u32[]{:S(2)}, u32[]{:S(2)}) collective-permute-start(bf16[272,512]{1,0:T(8,128)(2,1)} %inclusive.5.refs_0_), channel_id=1, source_target_pairs={{0,16},{4,20},{8,24},{12,28},{1,17},{5,21},{9,25},{13,29},{2,18},{... | collective-permute-start | bytes 835592 | tf_op jit(solution)/shard_map/ppermute | solution.py:560
  82.4 19.6 %collective-permute-start.8 = (bf16[272,512]{1,0:T(8,128)(2,1)}, bf16[272,512]{1,0:T(8,128)(2,1)}, u32[]{:S(2)}, u32[]{:S(2)}) collective-permute-start(bf16[272,512]{1,0:T(8,128)(2,1)} %get-tuple-element.87), channel_id=1, source_target_pairs={{0,8},{4,12},{8,16},{12,20},{16,24},{20,28},{1,9},{5,13},{9,17},{1... | collective-permute-start | bytes 835592 | tf_op jit(solution)/shard_map/ppermute | solution.py:560
  87.4 27.8 %collective-permute-start.13 = (bf16[256,1024]{1,0:T(8,128)(2,1)}, bf16[256,1024]{1,0:T(8,128)(2,1)}, u32[]{:S(2)}, u32[]{:S(2)}) collective-permute-start(bf16[256,1024]{1,0:T(8,128)(2,1)} %get-tuple-element.89.refs_6_), channel_id=1, source_target_pairs={{0,3},{1,2},{2,1},{3,0},{4,7},{5,6},{6,5},{7,4},{8,11},{9,10},{10,... | collective-permute-start | bytes 1572872 | tf_op jit(solution)/shard_map/ppermute | solution.py:672
  90.4 24.7 %collective-permute-start.14 = (bf16[256,1024]{1,0:T(8,128)(2,1)}, bf16[256,1024]{1,0:T(8,128)(2,1)}, u32[]{:S(2)}, u32[]{:S(2)}) collective-permute-start(bf16[256,1024]{1,0:T(8,128)(2,1)} %get-tuple-element.90.refs_0_), channel_id=1, source_target_pairs={{0,2},{1,3},{2,0},{3,1},{4,6},{5,7},{6,4},{7,5},{8,10},{9,11},{10,... | collective-permute-start | bytes 1572872 | tf_op jit(solution)/shard_map/ppermute | solution.py:672
  100.4 14.7 %collective-permute-start.12 = (bf16[256,512]{1,0:T(8,128)(2,1)S(1)}, bf16[256,512]{1,0:T(8,128)(2,1)S(1)}, u32[]{:S(2)}, u32[]{:S(2)}) collective-permute-start(bf16[256,512]{1,0:T(8,128)(2,1)S(1)} %get-tuple-element.94), channel_id=1, source_target_pairs={{0,4},{4,0},{8,12},{12,8},{16,20},{20,16},{24,28},{28,24},{1,5},{5... | collective-permute-start | bytes 786440 | tf_op jit(solution)/shard_map/ppermute | solution.py:568
  112.5 11.1 %collective-permute-start.11 = (bf16[272,512]{1,0:T(8,128)(2,1)S(1)}, bf16[272,512]{1,0:T(8,128)(2,1)S(1)}, u32[]{:S(2)}, u32[]{:S(2)}) collective-permute-start(bf16[272,512]{1,0:T(8,128)(2,1)S(1)} %get-tuple-element.93), channel_id=1, source_target_pairs={{0,4},{4,0},{8,12},{12,8},{16,20},{20,16},{24,28},{28,24},{1,5},{5... | collective-permute-start | bytes 835592 | tf_op jit(solution)/shard_map/ppermute | solution.py:568
  113.1 20.4 %collective-permute-start.15 = (bf16[272,512]{1,0:T(8,128)(2,1)}, bf16[272,512]{1,0:T(8,128)(2,1)}, u32[]{:S(2)}, u32[]{:S(2)}) collective-permute-start(bf16[272,512]{1,0:T(8,128)(2,1)} %inclusive.6.refs_0_), channel_id=1, source_target_pairs={{0,16},{4,20},{8,24},{12,28},{1,17},{5,21},{9,25},{13,29},{2,18},{... | collective-permute-start | bytes 835592 | tf_op jit(solution)/shard_map/ppermute | solution.py:560
  118.6 30.2 %collective-permute-start.19 = (bf16[272,1024]{1,0:T(8,128)(2,1)}, bf16[272,1024]{1,0:T(8,128)(2,1)}, u32[]{:S(2)}, u32[]{:S(2)}) collective-permute-start(bf16[272,1024]{1,0:T(8,128)(2,1)} %back_rest.3.refs_7_), channel_id=1, source_target_pairs={{0,3},{1,2},{2,1},{3,0},{4,7},{5,6},{6,5},{7,4},{8,11},{9,10},{10,... | collective-permute-start | bytes 1671176 | tf_op jit(solution)/shard_map/ppermute | solution.py:672
  123.1 25.7 %collective-permute-start.20 = (bf16[272,1024]{1,0:T(8,128)(2,1)}, bf16[272,1024]{1,0:T(8,128)(2,1)}, u32[]{:S(2)}, u32[]{:S(2)}) collective-permute-start(bf16[272,1024]{1,0:T(8,128)(2,1)} %back_rest.4.refs_0_), channel_id=1, source_target_pairs={{0,2},{1,3},{2,0},{3,1},{4,6},{5,7},{6,4},{7,5},{8,10},{9,11},{10,... | collective-permute-start | bytes 1671176 | tf_op jit(solution)/shard_map/ppermute | solution.py:672
  125.0 14.1 %collective-permute-start.17 = (bf16[272,512]{1,0:T(8,128)(2,1)}, bf16[272,512]{1,0:T(8,128)(2,1)}, u32[]{:S(2)}, u32[]{:S(2)}) collective-permute-start(bf16[272,512]{1,0:T(8,128)(2,1)} %get-tuple-element.101), channel_id=1, source_target_pairs={{0,8},{4,12},{8,16},{12,20},{16,24},{20,28},{1,9},{5,13},{9,17},{1... | collective-permute-start | bytes 835592 | tf_op jit(solution)/shard_map/ppermute | solution.py:560
  137.7 11.1 %collective-permute-start.16 = (bf16[256,512]{1,0:T(8,128)(2,1)}, bf16[256,512]{1,0:T(8,128)(2,1)}, u32[]{:S(2)}, u32[]{:S(2)}) collective-permute-start(bf16[256,512]{1,0:T(8,128)(2,1)} %get-tuple-element.100), channel_id=1, source_target_pairs={{0,4},{4,0},{8,12},{12,8},{16,20},{20,16},{24,28},{28,24},{1,5},{5... | collective-permute-start | bytes 786440 | tf_op jit(solution)/shard_map/ppermute | solution.py:568
  147.3 31.7 %copy-start.16 = (bf16[1024,128]{1,0:T(8,128)(2,1)S(1)}, bf16[1024,128]{1,0:T(8,128)(2,1)}, u32[]{:S(2)}) copy-start(bf16[1024,128]{1,0:T(8,128)(2,1)} %copy-done.14) | copy-start | bytes 786436
  147.3 8.1 %collective-permute-start.18 = (bf16[272,512]{1,0:T(8,128)(2,1)S(1)}, bf16[272,512]{1,0:T(8,128)(2,1)S(1)}, u32[]{:S(2)}, u32[]{:S(2)}) collective-permute-start(bf16[272,512]{1,0:T(8,128)(2,1)S(1)} %inclusive.7.refs_0_), channel_id=1, source_target_pairs={{0,16},{4,20},{8,24},{12,28},{1,17},{5,21},{9,25},{13,29},{2,18},{... | collective-permute-start | bytes 835592 | tf_op jit(solution)/shard_map/ppermute | solution.py:560
  153.5 13.9 %collective-permute-start.22 = (bf16[256,1024]{1,0:T(8,128)(2,1)S(1)}, bf16[256,1024]{1,0:T(8,128)(2,1)S(1)}, u32[]{:S(2)}, u32[]{:S(2)}) collective-permute-start(bf16[256,1024]{1,0:T(8,128)(2,1)S(1)} %get-tuple-element.102.refs_0_), channel_id=1, source_target_pairs={{0,3},{1,2},{2,1},{3,0},{4,7},{5,6},{6,5},{7,4},{8,11},{9,10},{10,... | collective-permute-start | bytes 1572872 | tf_op jit(solution)/shard_map/ppermute | solution.py:672
  154.0 25.0 %collective-permute-start.23 = (bf16[256,1024]{1,0:T(8,128)(2,1)S(1)}, bf16[256,1024]{1,0:T(8,128)(2,1)S(1)}, u32[]{:S(2)}, u32[]{:S(2)}) collective-permute-start(bf16[256,1024]{1,0:T(8,128)(2,1)S(1)} %get-tuple-element.106), channel_id=1, source_target_pairs={{0,2},{1,3},{2,0},{3,1},{4,6},{5,7},{6,4},{7,5},{8,10},{9,11},{10,... | collective-permute-start | bytes 1572872 | tf_op jit(solution)/shard_map/ppermute | solution.py:672
  155.5 30.7 %copy-start.18 = (bf16[1024,256]{1,0:T(8,128)(2,1)S(1)}, bf16[1024,256]{1,0:T(8,128)(2,1)}, u32[]{:S(2)}) copy-start(bf16[1024,256]{1,0:T(8,128)(2,1)} %copy-done.17) | copy-start | bytes 1572868
  155.5 30.6 %copy-start.20 = (bf16[256,512]{1,0:T(8,128)(2,1)S(1)}, bf16[256,512]{1,0:T(8,128)(2,1)}, u32[]{:S(2)}) copy-start(bf16[256,512]{1,0:T(8,128)(2,1)} %copy-done.19) | copy-start | bytes 786436
  155.5 30.6 %copy-start.22 = (bf16[256,512]{1,0:T(8,128)(2,1)S(1)}, bf16[256,512]{1,0:T(8,128)(2,1)}, u32[]{:S(2)}) copy-start(bf16[256,512]{1,0:T(8,128)(2,1)} %copy-done.21) | copy-start | bytes 786436
  155.5 30.6 %copy-start.24 = (bf16[256,512]{1,0:T(8,128)(2,1)S(1)}, bf16[256,512]{1,0:T(8,128)(2,1)}, u32[]{:S(2)}) copy-start(bf16[256,512]{1,0:T(8,128)(2,1)} %copy-done.23) | copy-start | bytes 786436
  155.5 30.6 %copy-start.26 = (bf16[256,512]{1,0:T(8,128)(2,1)S(1)}, bf16[256,512]{1,0:T(8,128)(2,1)}, u32[]{:S(2)}) copy-start(bf16[256,512]{1,0:T(8,128)(2,1)} %copy-done.25) | copy-start | bytes 786436
  157.1 29.1 %copy-start.5 = (f32[1024,1024]{1,0:T(8,128)S(1)}, f32[1024,1024]{1,0:T(8,128)}, u32[]{:S(2)}) copy-start(f32[1024,1024]{1,0:T(8,128)} %copy-done.4) | copy-start | bytes 12582916
  157.1 29.1 %copy-start.7 = (f32[1024,1024]{1,0:T(8,128)S(1)}, f32[1024,1024]{1,0:T(8,128)}, u32[]{:S(2)}) copy-start(f32[1024,1024]{1,0:T(8,128)} %copy-done.6) | copy-start | bytes 12582916
  157.1 8.2 %collective-permute-start.21 = (bf16[256,512]{1,0:T(8,128)(2,1)S(1)}, bf16[256,512]{1,0:T(8,128)(2,1)S(1)}, u32[]{:S(2)}, u32[]{:S(2)}) collective-permute-start(bf16[256,512]{1,0:T(8,128)(2,1)S(1)} %get-tuple-element.104), channel_id=1, source_target_pairs={{0,4},{4,0},{8,12},{12,8},{16,20},{20,16},{24,28},{28,24},{1,5},{5... | collective-permute-start | bytes 786440 | tf_op jit(solution)/shard_map/ppermute | solution.py:568
  192.5 27.2 %collective-permute-start.24 = (bf16[256,2048]{1,0:T(8,128)(2,1)}, bf16[256,2048]{1,0:T(8,128)(2,1)}, u32[]{:S(2)}, u32[]{:S(2)}) collective-permute-start(bf16[256,2048]{1,0:T(8,128)(2,1)} %get-tuple-element.109.refs_13_), channel_id=1, source_target_pairs={{0,1},{1,0},{2,3},{3,2},{4,5},{5,4},{6,7},{7,6},{8,9},{9,8},{10,11... | collective-permute-start | bytes 3145736 | tf_op jit(solution)/shard_map/ppermute | solution.py:672
  192.5 14.8 %collective-permute-start.26 = (bf16[272,1024]{1,0:T(8,128)(2,1)}, bf16[272,1024]{1,0:T(8,128)(2,1)}, u32[]{:S(2)}, u32[]{:S(2)}) collective-permute-start(bf16[272,1024]{1,0:T(8,128)(2,1)} %get-tuple-element.107.refs_12_), channel_id=1, source_target_pairs={{0,3},{1,2},{2,1},{3,0},{4,7},{5,6},{6,5},{7,4},{8,11},{9,10},{10,... | collective-permute-start | bytes 1671176 | tf_op jit(solution)/shard_map/ppermute | solution.py:672
  193.1 26.5 %collective-permute-start.27 = (bf16[272,1024]{1,0:T(8,128)(2,1)}, bf16[272,1024]{1,0:T(8,128)(2,1)S(1)}, u32[]{:S(2)}, u32[]{:S(2)}) collective-permute-start(bf16[272,1024]{1,0:T(8,128)(2,1)} %copy-done.66), channel_id=1, source_target_pairs={{0,2},{1,3},{2,0},{3,1},{4,6},{5,7},{6,4},{7,5},{8,10},{9,11},{10,... | collective-permute-start | bytes 1671176 | tf_op jit(solution)/shard_map/ppermute | solution.py:672
  207.2 22.4 %collective-permute-start.25 = (bf16[256,2048]{1,0:T(8,128)(2,1)S(1)}, bf16[256,2048]{1,0:T(8,128)(2,1)S(1)}, u32[]{:S(2)}, u32[]{:S(2)}) collective-permute-start(bf16[256,2048]{1,0:T(8,128)(2,1)S(1)} %get-tuple-element.111), channel_id=1, source_target_pairs={{0,1},{1,0},{2,3},{3,2},{4,5},{5,4},{6,7},{7,6},{8,9},{9,8},{10,11... | collective-permute-start | bytes 3145736 | tf_op jit(solution)/shard_map/ppermute | solution.py:672
  (65 other events, 529.7 us)
